TPU v7x, 512 devices: a whole 4x8x8 slice. The times are simulated.
512 devices in a mesh: grp: 8 (over z), dev: 64 (over x, y, core).
Axes of the slice: x: 4, y: 8, z: 8, core: 2. Of those that a mesh axis runs over, the one named last changes fastest.
Arguments:
- snapshots: float32 [262144, 128], P(('grp', 'dev')), may hold values from -16.5 to 16.5
- basis: float32 [262144, 128], P(('grp', 'dev')), may hold values from -1.4 to 1.4
Outputs:
- modes: float32 [262144, 128], P(('grp', 'dev'))
- factor: float32 [128, 128], replicated
- coefficients: float32 [128, 128], replicated
All inputs are finite; a program needn't handle non-finite values.
Results may differ from a plain program's by a relative error of at most 0.0003.
Values sent between devices are 32-bit elements; how exact they have to be, the bound alone decides.
No kernel may reach another device: no remote copies, remote signals or barrier semaphores. Data moves between devices by JAX's collectives and lax.ppermute only.
A program may use at most 64 MiB of HBM per device.

v0:
```python
import jax
import jax.numpy as jnp
from jax import lax
from jax.sharding import PartitionSpec as P


def cross_product(left, right):
    return jnp.einsum("rb,rk->bk", left, right, precision=lax.Precision.HIGHEST)


def apply_basis(basis, coef):
    return jnp.dot(basis, coef, precision=lax.Precision.HIGHEST)


def cholesky_upper(gram):
    size_n = gram.shape[0]
    column_ids = jnp.arange(size_n, dtype=jnp.int32)

    def column_step(step, carry):
        work, upper = carry
        row_vals = lax.dynamic_slice_in_dim(work, step, 1, 0)[0]
        pivot = jnp.sqrt(jnp.sum(jnp.where(column_ids == step, row_vals, 0.0)))
        row_new = jnp.where(column_ids >= step, row_vals / pivot, 0.0)
        upper = upper + jnp.where((column_ids == step)[:, None], row_new[None, :], 0.0)
        work = work - row_new[:, None] * row_new[None, :]
        return (work, upper)

    start = (gram, jnp.zeros_like(gram))
    return lax.fori_loop(0, size_n, column_step, start)[1]


def upper_inverse(gram):
    upper_part = cholesky_upper(gram)
    size_n = gram.shape[0]
    column_ids = jnp.arange(size_n, dtype=jnp.int32)

    def row_step(turn, inverse):
        row_at = size_n - 1 - turn
        row_vals = lax.dynamic_slice_in_dim(upper_part, row_at, 1, 0)[0]
        diag_val = jnp.sum(jnp.where(column_ids == row_at, row_vals, 0.0))
        off_diag = jnp.where(column_ids > row_at, row_vals, 0.0)
        unit_row = jnp.where(column_ids == row_at, 1.0, 0.0).astype(gram.dtype)
        new_row = (
            unit_row - jnp.dot(off_diag, inverse, precision=lax.Precision.HIGHEST)
        ) / diag_val
        return inverse + jnp.where((column_ids == row_at)[:, None], new_row[None, :], 0.0)

    inverse = lax.fori_loop(0, size_n, row_step, jnp.zeros_like(gram))
    return (upper_part, inverse)


def total_gram(local_part):
    return lax.psum(local_part, ("grp", "dev"))


def body(snapshots, basis):
    total_rows = snapshots.shape[0] * lax.axis_size("grp") * lax.axis_size("dev")
    coef_one = lax.psum(cross_product(basis, snapshots), ("grp", "dev")) / total_rows
    first = snapshots - apply_basis(basis, coef_one)
    coef_two = lax.psum(cross_product(basis, first), ("grp", "dev")) / total_rows
    second = first - apply_basis(basis, coef_two)
    gram_one = total_gram(cross_product(second, second)) / total_rows
    upper_one, inv_one = upper_inverse(gram_one)
    middle = apply_basis(second, inv_one)
    gram_two = total_gram(cross_product(middle, middle)) / total_rows
    upper_two, inv_two = upper_inverse(gram_two)
    modes = apply_basis(middle, inv_two)
    factor = jnp.dot(upper_two, upper_one, precision=lax.Precision.HIGHEST)
    return (modes, factor, coef_one + coef_two)


def solution(mesh):
    return jax.shard_map(
        body,
        mesh=mesh,
        in_specs=(P(("grp", "dev"), None), P(("grp", "dev"), None)),
        out_specs=(P(("grp", "dev"), None), P(), P()),
        check_vma=False,
    )
```

profile of v0, /device:TPU:1, one launch (start us, length us, event | category | flops | bytes accessed | tf_op | source)
XLA Modules:
  0.0 1835.9 jit_solution(17066007041721607587)
XLA Ops:
  7.2 0.9 copy-done
  8.1 2.2 fusion.44
  10.5 267.6 %all-reduce.5.cloned.1.call-done = f32[128,128]{1,0:T(8,128)} async-done(((f32[128,128]{1,0:T(8,128)}), f32[128,128]{1,0:T(8,128)}) %all-reduce.5.cloned.1.call-update) | async-done | bytes 65552 | tf_op jit(solution)/shard_map/psum | solution.py:58
  278.1 1.3 fusion.37
  279.4 1.2 convolution_bitcast_fusion.4
  280.7 255.0 %all-reduce.7.cloned.1.call-done = f32[128,128]{1,0:T(8,128)} async-done(((f32[128,128]{1,0:T(8,128)}), f32[128,128]{1,0:T(8,128)}) %all-reduce.7.cloned.1.call-update) | async-done | bytes 65552 | tf_op jit(solution)/shard_map/psum | solution.py:60
  535.7 1.3 fusion.36
  537.0 1.0 fusion.45
  538.1 254.5 %all-reduce.9.cloned.1.call-done = f32[128,128]{1,0:T(8,128)} async-done(((f32[128,128]{1,0:T(8,128)}), f32[128,128]{1,0:T(8,128)}) %all-reduce.9.cloned.1.call-update) | async-done | bytes 65552 | tf_op jit(solution)/shard_map/psum | solution.py:53
  792.6 0.8 broadcast_multiply_fusion.1
  793.4 191.3 %while.68 = (s32[]{:T(128)}, f32[128,128]{1,0:T(8,128)S(1)}, f32[128,128]{1,0:T(8,128)S(1)}, s32[]{:T(128)}, s32[]{:T(128)}) while((s32[]{:T(128)}, f32[128,128]{1,0:T(8,128)S(1)}, f32[128,128]{1,0:T(8,128)S(1)}, s32[]{:T(128)}, s32[]{:T(128)}) %tuple.151), condition=%wide.region_5.6_spmd.clone.clone, body=%wide.region_3.5_spmd.clone.clone.sunk | while | flops 83202 | bytes 269151 | solution.py:29
  984.8 198.6 %while.69 = (s32[]{:T(128)}, f32[128,128]{1,0:T(8,128)S(1)}, f32[128,128]{1,0:T(8,128)S(1)}, s32[]{:T(128)}, s32[]{:T(128)}, /*index=5*/s32[]{:T(128)}, s32[]{:T(128)}) while((s32[]{:T(128)}, f32[128,128]{1,0:T(8,128)S(1)}, f32[128,128]{1,0:T(8,128)S(1)}, s32[]{:T(128)}, s32[]{:T(128)}, /*index=5*/s32[]{:T(128)}, ...), condition=%wide.region_8.9_spmd.clone.clone, body=%wide.region_6.8_spmd.clone.clone.sunk | while | flops 263430 | bytes 201113 | solution.py:48
  985.4 0.8 fusion.83
  986.9 0.8 fusion.83
  988.5 0.8 fusion.83
  990.0 0.8 fusion.83
  991.6 0.8 fusion.83
  993.1 0.8 fusion.83
  994.7 0.8 fusion.83
  1014.9 0.8 fusion.83
  1016.4 0.8 fusion.83
  1018.0 0.8 fusion.83
  1019.5 0.8 fusion.83
  1021.1 0.8 fusion.83
  1022.6 0.8 fusion.83
  1024.2 0.8 fusion.83
  1044.3 0.8 fusion.83
  1045.9 0.8 fusion.83
  1047.5 0.8 fusion.83
  1049.0 0.8 fusion.83
  1050.6 0.8 fusion.83
  1052.1 0.8 fusion.83
  1053.7 0.8 fusion.83
  1073.8 0.8 fusion.83
  1075.4 0.8 fusion.83
  1076.9 0.8 fusion.83
  1078.5 0.8 fusion.83
  1080.0 0.8 fusion.83
  1081.6 0.8 fusion.83
  1083.1 0.8 fusion.83
  1184.0 1.2 fusion.47
  1185.2 0.8 copy-done.2
  1186.7 250.0 %all-reduce.11.cloned.1.call-done = f32[128,128]{1,0:T(8,128)} async-done(((f32[128,128]{1,0:T(8,128)}), f32[128,128]{1,0:T(8,128)}) %all-reduce.11.cloned.1.call-update) | async-done | bytes 65552 | tf_op jit(solution)/shard_map/psum | solution.py:53
  1436.7 0.8 broadcast_multiply_fusion
  1437.5 191.3 %while.70 = (s32[]{:T(128)}, f32[128,128]{1,0:T(8,128)S(1)}, f32[128,128]{1,0:T(8,128)S(1)}, s32[]{:T(128)}, s32[]{:T(128)}) while((s32[]{:T(128)}, f32[128,128]{1,0:T(8,128)S(1)}, f32[128,128]{1,0:T(8,128)S(1)}, s32[]{:T(128)}, s32[]{:T(128)}) %tuple.157), condition=%wide.region_12.13_spmd.clone.clone, body=%wide.region_10.12_spmd.clone.clone.sunk | while | flops 83202 | bytes 269151 | solution.py:29
  1628.9 0.8 fusion.49
  1629.7 198.6 %while.71 = (s32[]{:T(128)}, f32[128,128]{1,0:T(8,128)S(1)}, f32[128,128]{1,0:T(8,128)S(1)}, s32[]{:T(128)}, s32[]{:T(128)}, /*index=5*/s32[]{:T(128)}, s32[]{:T(128)}) while((s32[]{:T(128)}, f32[128,128]{1,0:T(8,128)S(1)}, f32[128,128]{1,0:T(8,128)S(1)}, s32[]{:T(128)}, s32[]{:T(128)}, /*index=5*/s32[]{:T(128)}, ...), condition=%wide.region_15.16_spmd.clone.clone, body=%wide.region_13.15_spmd.clone.clone.sunk | while | flops 263430 | bytes 201113 | solution.py:48
  1828.3 1.1 fusion.48
  (2297 shorter events, 559.3 us)
Async XLA Ops:
  7.2 1.0 copy-start
  7.2 3.2 copy-start.1
  7.2 270.9 %all-reduce.5.cloned.1.call-start = ((), (), s32[]{:S(2)}) async-start(), calls=%async_computation | async-start | bytes 131072 | tf_op jit(solution)/shard_map/psum | solution.py:58
  10.3 525.4 %all-reduce.7.cloned.1.call-start = ((), (), s32[]{:S(2)}) async-start(), calls=%async_computation.1 | async-start | bytes 131072 | tf_op jit(solution)/shard_map/psum | solution.py:60
  280.6 512.0 %all-reduce.9.cloned.1.call-start = ((), (), s32[]{:S(2)}) async-start(), calls=%async_computation.2 | async-start | bytes 131072 | tf_op jit(solution)/shard_map/psum | solution.py:53
  538.0 898.7 %all-reduce.11.cloned.1.call-start = ((), (), s32[]{:S(2)}) async-start(), calls=%async_computation.3 | async-start | bytes 131072 | tf_op jit(solution)/shard_map/psum | solution.py:53
  1184.0 1.3 copy-start.3
  1185.2 0.8 copy-start.2
Sparse Core Ops, SparseCore 0:
  13.6 264.5 all-reduce.4
  284.5 251.2 all-reduce.6
  541.3 251.2 all-reduce.8
  1185.3 251.3 all-reduce.10
where the time goes:
time: 1840 us
  waiting for transfers between devices  1030 us (56%)
  other arithmetic  378 us (21%)
  matrix products  215 us (12%)
  loops' own time  200 us (11%)
    psum x2, waiting for transfers between devices, total_gram(): return lax.psum(local_part, ('grp', 'dev'))  504 us
    psum x1, waiting for transfers between devices, body(): lax.psum(cross_product(basis, snapshots), ('grp', 'dev')) / total_rows  268 us
    psum x1, waiting for transfers between devices, body(): lax.psum(cross_product(basis, first), ('grp', 'dev')) / total_rows  255 us
    dot_general x256, matrix products, row_step(): jnp.dot(off_diag, inverse, precision=lax.Precision.HIGHEST)  205 us
    another operation x2, loops' own time, cholesky_upper(): return lax.fori_loop(0, size_n, column_step, start)[1]  190 us
    reduce_sum x256, other arithmetic, row_step(): diag_val = jnp.sum(jnp.where(column_ids == row_at, row_vals, 0.0))  155 us
    reduce_sum x256, other arithmetic, column_step(): pivot = jnp.sqrt(jnp.sum(jnp.where(column_ids == step, row_vals, 0.0)))  155 us
  transfers between devices with their start and end apart: 4, of which 4 were waited for; matrix products, arithmetic and copies ran while one was open for 0% of the time, Pallas kernels for 0%

commit v1 on v0

v1 whole, which is shorter than its diff:
```python
import functools

import jax
import jax.numpy as jnp
from jax import lax
from jax.experimental import pallas as pl
from jax.experimental.pallas import tpu as pltpu
from jax.sharding import PartitionSpec as P

HIGHEST = lax.Precision.HIGHEST
F32, BF16 = jnp.float32, jnp.bfloat16
N = 128
TILE = 8
TILES = N // TILE
PIECE = 2 * TILE


def two_sum(a, b):
    s = a + b
    t = s - a
    return s, (a - (s - t)) + (b - t)


def pair_sum(a, b):
    s, e = two_sum(a[0], b[0])
    return s, e + (a[1] + b[1])


def normal(a):
    s = a[0] + a[1]
    return s, a[1] - (s - a[0])


def dot_t(a, b, precision=None):
    return lax.dot_general(
        a, b, (((0,), (0,)), ((), ())), precision=precision, preferred_element_type=F32
    )


def dot(a, b, precision=None):
    return jnp.dot(a, b, precision=precision, preferred_element_type=F32)


def slices(hi, lo, axis, count, shift):
    step = jnp.max(jnp.abs(hi), axis=axis, keepdims=True) * (2.0**shift)
    first = (hi + step) - step
    rest = hi - first
    step = step * 2.0**-8
    second = (rest + step) - step
    rest = rest - second
    if lo is not None:
        rest = rest + lo
    out = [first.astype(BF16), second.astype(BF16)]
    while len(out) < count:
        part = rest.astype(BF16)
        rest = rest - part.astype(F32)
        out.append(part)
    return out


def exact_dot(left, right):
    wide = jnp.concatenate(left, axis=1)
    tall = jnp.concatenate(right[::-1], axis=0)
    n = len(left)
    terms = [dot(wide[:, : N * k], tall[N * (n - k) :, :]) for k in range(1, n + 1)]
    low = terms[-1]
    for t in terms[-2:1:-1]:
        low = low + t
    s, e = two_sum(terms[0], terms[1])
    return s, e + low


def local_kernel(snap_ref, basis_ref, out_ref):
    z = jnp.concatenate([basis_ref[...], snap_ref[...]], axis=1)
    a, b, c, d = slices(z, None, 0, 4, 17)
    main = dot_t(a, a)
    low_1 = dot_t(a, b)
    low_2 = dot_t(a, c) + 0.5 * dot_t(b, b)
    low_3 = dot_t(a, d) + dot_t(b, c)
    low_4 = dot_t(b, d) + 0.5 * dot_t(c, c)
    half = low_1 + (low_2 + (low_3 + low_4))
    hi, lo = two_sum(main, half + half.T)
    scale = 2.0**-18
    blocks = ((0, 0), (0, 1), (1, 1))
    for i, (r, s) in enumerate(blocks):
        for j, part in enumerate((hi, lo)):
            block = part[r * N : (r + 1) * N, s * N : (s + 1) * N]
            out_ref[i * TILES : (i + 1) * TILES, j * TILE : (j + 1) * TILE, :] = (
                block * scale
            ).reshape(TILES, TILE, N)
    used = len(blocks) * TILES
    out_ref[used:, :, :] = jnp.zeros_like(out_ref[used:, :, :])


def local_products(snapshots, basis, pieces):
    return pl.pallas_call(
        local_kernel,
        out_shape=jax.ShapeDtypeStruct((pieces, PIECE, N), F32),
        compiler_params=pltpu.CompilerParams(vmem_limit_bytes=32 << 20),
    )(snapshots, basis)


def sum_kernel(in_ref, out_ref):
    parts = [(in_ref[i, :TILE, :], in_ref[i, TILE:, :]) for i in range(in_ref.shape[0])]
    while len(parts) > 1:
        parts = [pair_sum(parts[i], parts[i + 1]) for i in range(0, len(parts), 2)]
    hi, lo = parts[0]
    for i in range(out_ref.shape[0]):
        out_ref[i, :TILE, :] = hi
        out_ref[i, TILE:, :] = lo


def sum_and_copy(parts, copies):
    return pl.pallas_call(
        sum_kernel,
        out_shape=jax.ShapeDtypeStruct((copies, PIECE, N), F32),
        compiler_params=pltpu.CompilerParams(vmem_limit_bytes=32 << 20),
    )(parts)


def factor_inverse(gram, scratch):
    sub = lax.broadcasted_iota(jnp.int32, (TILE, N), 0)
    lane = lax.broadcasted_iota(jnp.int32, (TILE, N), 1)
    work = gram
    inv = jnp.where(
        lax.broadcasted_iota(jnp.int32, (N, N), 0)
        == lax.broadcasted_iota(jnp.int32, (N, N), 1),
        1.0,
        0.0,
    ).astype(F32)
    upper_rows, inv_rows = [], []
    for p in range(TILES):
        at = p * TILE
        rows = work[:TILE, :]
        irow = inv[:TILE, :]
        d = {}
        for j in range(TILE):
            col = jnp.broadcast_to(rows[:, at + j : at + j + 1], (TILE, N))
            for i in range(j + 1):
                d[i, j] = jnp.broadcast_to(col[i : i + 1, :], (TILE, N))
        r = []
        for k in range(TILE):
            piv = d[k, k]
            y = lax.rsqrt(piv)
            y = y * (1.5 - 0.5 * piv * y * y)
            r.append(y)
            for j in range(k + 1, TILE):
                d[k, j] = d[k, j] * y
            for i in range(k + 1, TILE):
                for j in range(i, TILE):
                    d[i, j] = d[i, j] - d[k, i] * d[k, j]
        li = {}
        for j in range(TILE):
            li[j, j] = r[j]
            for i in range(j + 1, TILE):
                acc = d[j, i] * li[j, j]
                for k in range(j + 1, i):
                    acc = acc + d[k, i] * li[k, j]
                li[i, j] = -(acc * r[i])
        new_u = jnp.zeros((TILE, N), F32)
        new_i = jnp.zeros((TILE, N), F32)
        for k in range(TILE):
            colk = jnp.zeros((TILE, N), F32)
            for i in range(k, TILE):
                colk = jnp.where(sub == i, li[i, k], colk)
            new_u = new_u + colk * jnp.broadcast_to(rows[k : k + 1, :], (TILE, N))
            new_i = new_i + colk * jnp.broadcast_to(irow[k : k + 1, :], (TILE, N))
        new_u = jnp.where(lane >= at + sub, new_u, 0.0)
        upper_rows.append(new_u)
        inv_rows.append(new_i)
        if p + 1 < TILES:
            both = jnp.concatenate([new_u, new_i], axis=1)
            b1 = both.astype(BF16)
            rest = both - b1.astype(F32)
            b2 = rest.astype(BF16)
            b3 = (rest - b2.astype(F32)).astype(BF16)
            f1, f2, f3 = b1.astype(F32), b2.astype(F32), b3.astype(F32)
            left = jnp.concatenate([f[:, :N] for f in (f1, f1, f2, f1, f2, f3)], axis=0)
            right = jnp.concatenate([f1, f2, f1, f3, f2, f1], axis=0).astype(BF16)
            left = left.T.astype(BF16)[at + TILE :, :]
            upd = dot(left, right)
            work = work[TILE:, :] - upd[:, :N]
            inv = inv[TILE:, :] - upd[:, N:]
    return jnp.concatenate(upper_rows, axis=0), jnp.concatenate(inv_rows, axis=0)


def final_kernel(sums_ref, snap_ref, basis_ref, modes_ref, factor_ref, coef_ref, scratch):
    def pair(i):
        part = sums_ref[i * TILES : (i + 1) * TILES, :, :]
        return part[:, :TILE, :].reshape(N, N), part[:, TILE:, :].reshape(N, N)

    basis_gram, cross, snap_gram = pair(0), pair(1), pair(2)
    coef_two = cross[0] - dot(basis_gram[0], cross[0], HIGHEST)
    coef = cross[0] + coef_two
    coef_ref[...] = coef
    second = snap_ref[...] - dot(basis_ref[...], coef, HIGHEST)

    g_c = exact_dot(slices(*basis_gram, 1, 5, 16), slices(coef, None, 0, 5, 16))
    held = pair_sum((2.0 * cross[0], 2.0 * cross[1]), (-g_c[0], -g_c[1]))
    held = normal(held)
    c_h = exact_dot(slices(coef.T, None, 1, 5, 16), slices(*held, 0, 5, 16))
    c_h = pair_sum((0.5 * c_h[0], 0.5 * c_h[1]), (0.5 * c_h[0].T, 0.5 * c_h[1].T))
    gram_one = normal(pair_sum(snap_gram, (-c_h[0], -c_h[1])))

    upper_one, inv_one_t = factor_inverse(gram_one[0], scratch)
    inv_one = inv_one_t.T
    g_i = exact_dot(slices(*gram_one, 1, 5, 16), slices(inv_one, None, 0, 5, 16))
    g_i = normal(g_i)
    i_g_i = exact_dot(slices(inv_one_t, None, 1, 5, 16), slices(*g_i, 0, 5, 16))
    gram_two = i_g_i[0] + i_g_i[1]
    upper_two, inv_two_t = factor_inverse(gram_two, scratch)
    factor_ref[...] = dot(upper_two, upper_one, HIGHEST)
    both = dot(inv_one, inv_two_t.T, HIGHEST)
    modes_ref[...] = dot(second, both, HIGHEST)


def finish(sums, snapshots, basis):
    rows = snapshots.shape[0]
    return pl.pallas_call(
        final_kernel,
        out_shape=(
            jax.ShapeDtypeStruct((rows, N), F32),
            jax.ShapeDtypeStruct((N, N), F32),
            jax.ShapeDtypeStruct((N, N), F32),
        ),
        scratch_shapes=[pltpu.VMEM((N, N), F32)],
        compiler_params=pltpu.CompilerParams(vmem_limit_bytes=48 << 20),
    )(sums, snapshots, basis)


def body(snapshots, basis):
    group, many = lax.axis_size("grp"), lax.axis_size("dev")
    local = local_products(snapshots, basis, many)
    parts = lax.all_to_all(local, "dev", 0, 0)
    mine = sum_and_copy(parts, group)
    parts = lax.all_to_all(mine, "grp", 0, 0)
    mine = sum_and_copy(parts, many)
    sums = lax.all_to_all(mine, "dev", 0, 0)
    return finish(sums, snapshots, basis)


def solution(mesh):
    return jax.shard_map(
        body,
        mesh=mesh,
        in_specs=(P(("grp", "dev"), None), P(("grp", "dev"), None)),
        out_specs=(P(("grp", "dev"), None), P(), P()),
        check_vma=False,
    )
```

time: 1840 us -> 91.6 us (0.05)
  waiting for transfers between devices: 1030 us -> 0 us
  other arithmetic: 378 us -> 0 us
  matrix products: 215 us -> 0 us
  loops' own time: 200 us -> 0 us
  blocking collectives: 0 us -> 70.8 us
    psum x4 -> x0, waiting for transfers between devices: 1030 us -> none  [the longest x2 504 us: total_gram(): return lax.psum(local_part, ('grp', 'dev'))]
    reduce_sum x512 -> x0, other arithmetic: 311 us -> none  [the longest x256 155 us: row_step(): diag_val = jnp.sum(jnp.where(column_ids == row_at, row_vals, 0.0))]
    dot_general x265 -> x0, matrix products: 215 us -> none  [the longest x256 205 us: row_step(): jnp.dot(off_diag, inverse, precision=lax.Precision.HIGHEST)]
    another operation x4 -> x0, loops' own time: 200 us -> none  [the longest x2 190 us: cholesky_upper(): return lax.fori_loop(0, size_n, column_step, start)[1]]
    all_to_all x0 -> x3, blocking collectives: none -> 70.8 us  [the longest x1 28.7 us: body(): parts = lax.all_to_all(local, 'dev', 0, 0)]
    add x513 -> x0, other arithmetic: 52.8 us -> none  [the longest x256 29 us: column_step(): upper + jnp.where((column_ids == step)[:, None], row_new[None, :], 0.0)]
  transfers between devices with their start and end apart: 4 -> 0, of which waited for: 4 -> 0; matrix products, arithmetic and copies ran while one was open for 0% -> 0% of each run, Pallas kernels for 0% -> 0%
where the time goes in v1:
time: 91.6 us; the launch traced here: 91.3 us
  blocking collectives  70.8 us (77%)
  Pallas kernels  18 us (20%)
  local copies, waits for them, and re-layouts  1.91 us (2%)
    all_to_all x1, blocking collectives, body(): parts = lax.all_to_all(local, 'dev', 0, 0)  28.7 us
    all_to_all x1, blocking collectives, body(): sums = lax.all_to_all(mine, 'dev', 0, 0)  25 us
    all_to_all x1, blocking collectives, body(): parts = lax.all_to_all(mine, 'grp', 0, 0)  17.1 us
    pallas_call x1, Pallas kernels, finish(): pl.pallas_call(final_kernel, out_shape=(jax.ShapeDtypeStruct((rows, N), F...  16.9 us
    unnamed x8, local copies, waits for them, and re-layouts  1.91 us

profile of v1, /device:TPU:1, one launch (start us, length us, event | category | flops | bytes accessed | tf_op | source)
XLA Modules:
  0.0 91.3 jit_solution(4292167489984725194)
XLA Ops:
  0.6 0.0 copy-start
  0.6 0.9 %copy-done = f32[512,128]{1,0:T(8,128)S(1)} copy-done((f32[512,128]{1,0:T(8,128)S(1)}, f32[512,128]{1,0:T(8,128)}, u32[]{:S(2)}) %copy-start) | copy-done | bytes 262168
  1.6 0.0 copy-start.2
  1.6 0.9 %copy-done.2 = f32[512,128]{1,0:T(8,128)S(1)} copy-done((f32[512,128]{1,0:T(8,128)S(1)}, f32[512,128]{1,0:T(8,128)}, u32[]{:S(2)}) %copy-start.2) | copy-done | bytes 262168
  2.5 0.9 %shard_map.49 = f32[64,16,128]{2,1,0:T(8,128)S(1)} custom-call(f32[512,128]{1,0:T(8,128)S(1)} %copy-done, f32[512,128]{1,0:T(8,128)S(1)} %copy-done.2), custom_call_target="tpu_custom_call" | custom-call | tf_op jit(solution)/shard_map/pallas_call | solution.py:96
  3.5 28.7 %all_to_all.15.in_ref = f32[64,16,128]{2,1,0:T(8,128)S(1)} all-to-all(f32[64,16,128]{2,1,0:T(8,128)S(1)} %shard_map.49), channel_id=1, replica_groups=mesh['grp'=8,'dev'=64] {'dev'}, dimensions={0} | all-to-all | bytes 1048576 | tf_op jit(solution)/shard_map/all_to_all | solution.py:234
  32.2 0.1 shard_map.50
  32.3 17.1 %all_to_all.16.in_ref = f32[8,16,128]{2,1,0:T(8,128)S(1)} all-to-all(f32[8,16,128]{2,1,0:T(8,128)S(1)} %shard_map.50), channel_id=1, replica_groups=mesh['grp'=8,'dev'=64] {'grp'}, dimensions={0} | all-to-all | bytes 131072 | tf_op jit(solution)/shard_map/all_to_all | solution.py:236
  49.4 0.0 copy-start.1
  49.4 0.0 copy-start.3
  49.4 25.0 %all_to_all.17.sums_ref = f32[64,16,128]{2,1,0:T(8,128)S(1)} all-to-all(f32[64,16,128]{2,1,0:T(8,128)S(1)} %shard_map.51), channel_id=1, replica_groups=mesh['grp'=8,'dev'=64] {'dev'}, dimensions={0} | all-to-all | bytes 1048576 | tf_op jit(solution)/shard_map/all_to_all | solution.py:238
  74.4 0.0 copy-done.1
  74.4 0.0 copy-done.3
  74.4 16.9 %shard_map.52 = (f32[512,128]{1,0:T(8,128)}, f32[128,128]{1,0:T(8,128)}, f32[128,128]{1,0:T(8,128)}) custom-call(f32[64,16,128]{2,1,0:T(8,128)S(1)} %all_to_all.17.sums_ref, f32[512,128]{1,0:T(8,128)S(1)} %copy-done.1, f32[512,128]{1,0:T(8,128)S(1)} %copy-done.3), custom_call_target="tpu_custom_call" | custom-call | tf_op jit(solution)/shard_map/pallas_call | solution.py:219
  (1 shorter events, 0.0 us)
Async XLA Ops:
  0.6 1.0 %copy-start = (f32[512,128]{1,0:T(8,128)S(1)}, f32[512,128]{1,0:T(8,128)}, u32[]{:S(2)}) copy-start(f32[512,128]{1,0:T(8,128)} %snap_ref.3) | copy-start | bytes 786436
  1.6 0.9 %copy-start.2 = (f32[512,128]{1,0:T(8,128)S(1)}, f32[512,128]{1,0:T(8,128)}, u32[]{:S(2)}) copy-start(f32[512,128]{1,0:T(8,128)} %basis_ref.3) | copy-start | bytes 786436
  49.4 25.0 %copy-start.1 = (f32[512,128]{1,0:T(8,128)S(1)}, f32[512,128]{1,0:T(8,128)}, u32[]{:S(2)}) copy-start(f32[512,128]{1,0:T(8,128)} %snap_ref.3) | copy-start | bytes 786436
  49.4 25.0 %copy-start.3 = (f32[512,128]{1,0:T(8,128)S(1)}, f32[512,128]{1,0:T(8,128)}, u32[]{:S(2)}) copy-start(f32[512,128]{1,0:T(8,128)} %basis_ref.3) | copy-start | bytes 786436

commit v2 on v1

--- a/solution.py
+++ b/solution.py
@@ -12,7 +12,6 @@
 N = 128
 TILE = 8
 TILES = N // TILE
-PIECE = 2 * TILE
 
 
 def two_sum(a, b):
@@ -70,9 +69,62 @@
     return s, e + low
 
 
-def local_kernel(snap_ref, basis_ref, out_ref):
-    z = jnp.concatenate([basis_ref[...], snap_ref[...]], axis=1)
-    a, b, c, d = slices(z, None, 0, 4, 17)
+def grid(rows=N):
+    return (
+        lax.broadcasted_iota(jnp.int32, (rows, N), 0),
+        lax.broadcasted_iota(jnp.int32, (rows, N), 1),
+    )
+
+
+def put_diagonal(rest, diagonal):
+    row, col = grid(N // 2)
+    near = pltpu.roll(diagonal[N // 2 :, :], N - N // 4, 1)
+    far = pltpu.roll(diagonal[: N // 2, :], N // 2, 1)
+    top = jnp.where(col == row + N // 4, near, rest[: N // 2, :])
+    top = jnp.where(col == row + N // 2, far, top)
+    return jnp.concatenate([top, rest[N // 2 :, :]], axis=0)
+
+
+def take_diagonal(rest):
+    row, col = grid(N // 2)
+    top = rest[: N // 2, :]
+    near, far = col == row + N // 4, col == row + N // 2
+    first = pltpu.roll(jnp.where(far, top, 0.0), N // 2, 1)
+    last = pltpu.roll(jnp.where(near, top, 0.0), N // 4, 1)
+    top = jnp.where(near | far, 0.0, top)
+    return (
+        jnp.concatenate([first, last], axis=0),
+        jnp.concatenate([top, rest[N // 2 :, :]], axis=0),
+    )
+
+
+def pack(hi, lo):
+    hi, lo = hi.reshape(TILES, TILE, N), lo.reshape(TILES, TILE, N)
+    upper = lax.broadcasted_iota(jnp.int32, hi.shape, 1) < TILE // 2
+    even = jnp.where(upper, hi, pltpu.roll(lo, TILE // 2, 1))
+    odd = jnp.where(upper, pltpu.roll(hi, TILE // 2, 1), lo)
+    return jnp.stack([even, odd], axis=1).reshape(2 * TILES, TILE, N)
+
+
+def unpack(pieces):
+    pieces = pieces.reshape(TILES, 2, TILE, N)
+    even, odd = pieces[:, 0], pieces[:, 1]
+    upper = lax.broadcasted_iota(jnp.int32, even.shape, 1) < TILE // 2
+    hi = jnp.where(upper, even, pltpu.roll(odd, TILE // 2, 1))
+    lo = jnp.where(upper, pltpu.roll(even, TILE // 2, 1), odd)
+    return hi.reshape(N, N), lo.reshape(N, N)
+
+
+def local_kernel(share, total, snap_hbm, basis_hbm, out_ref, z_ref, sem):
+    copies = [
+        pltpu.make_async_copy(basis_hbm, z_ref.at[:, :N], sem.at[0]),
+        pltpu.make_async_copy(snap_hbm, z_ref.at[:, N:], sem.at[1]),
+    ]
+    for copy in copies:
+        copy.start()
+    for copy in copies:
+        copy.wait()
+    a, b, c, d = slices(z_ref[...], None, 0, 4, 17)
     main = dot_t(a, a)
     low_1 = dot_t(a, b)
     low_2 = dot_t(a, c) + 0.5 * dot_t(b, b)
@@ -80,45 +132,53 @@
     low_4 = dot_t(b, d) + 0.5 * dot_t(c, c)
     half = low_1 + (low_2 + (low_3 + low_4))
     hi, lo = two_sum(main, half + half.T)
-    scale = 2.0**-18
-    blocks = ((0, 0), (0, 1), (1, 1))
-    for i, (r, s) in enumerate(blocks):
-        for j, part in enumerate((hi, lo)):
-            block = part[r * N : (r + 1) * N, s * N : (s + 1) * N]
-            out_ref[i * TILES : (i + 1) * TILES, j * TILE : (j + 1) * TILE, :] = (
-                block * scale
-            ).reshape(TILES, TILE, N)
-    used = len(blocks) * TILES
-    out_ref[used:, :, :] = jnp.zeros_like(out_ref[used:, :, :])
-
-
-def local_products(snapshots, basis, pieces):
+    hi, lo = hi * (1.0 / total), lo * (1.0 / total)
+    row, col = grid()
+    diagonal = jnp.where(row == col, (hi[:N, :N] - share) + lo[:N, :N], 0.0)
+    mixed_hi = jnp.where(row < col, hi[:N, :N], hi[N:, N:])
+    mixed_lo = put_diagonal(jnp.where(row < col, lo[:N, :N], lo[N:, N:]), diagonal)
+    out_ref[: 2 * TILES] = pack(mixed_hi, mixed_lo)
+    out_ref[2 * TILES :] = pack(hi[:N, N:], lo[:N, N:])
+
+
+def local_products(snapshots, basis, devices):
+    rows = snapshots.shape[0]
+    total = rows * devices
     return pl.pallas_call(
-        local_kernel,
-        out_shape=jax.ShapeDtypeStruct((pieces, PIECE, N), F32),
+        functools.partial(local_kernel, 1.0 / devices, total),
+        out_shape=jax.ShapeDtypeStruct((4 * TILES, TILE, N), F32),
+        in_specs=[pl.BlockSpec(memory_space=pltpu.HBM)] * 2,
+        scratch_shapes=[pltpu.VMEM((rows, 2 * N), F32), pltpu.SemaphoreType.DMA((2,))],
         compiler_params=pltpu.CompilerParams(vmem_limit_bytes=32 << 20),
     )(snapshots, basis)
 
 
 def sum_kernel(in_ref, out_ref):
-    parts = [(in_ref[i, :TILE, :], in_ref[i, TILE:, :]) for i in range(in_ref.shape[0])]
+    parts = [(in_ref[i], None) for i in range(in_ref.shape[0])]
     while len(parts) > 1:
-        parts = [pair_sum(parts[i], parts[i + 1]) for i in range(0, len(parts), 2)]
-    hi, lo = parts[0]
+        added = []
+        for (a, a_left), (b, b_left) in zip(parts[::2], parts[1::2]):
+            s, left = two_sum(a, b)
+            if a_left is not None:
+                left = left + (a_left + b_left)
+            added.append((s, left))
+        parts = added
+    s, left = parts[0]
+    lower = lax.broadcasted_iota(jnp.int32, s.shape, 0) >= TILE // 2
+    s = s + jnp.where(lower, pltpu.roll(left, TILE // 2, 0), 0.0)
     for i in range(out_ref.shape[0]):
-        out_ref[i, :TILE, :] = hi
-        out_ref[i, TILE:, :] = lo
+        out_ref[i] = s
 
 
 def sum_and_copy(parts, copies):
     return pl.pallas_call(
         sum_kernel,
-        out_shape=jax.ShapeDtypeStruct((copies, PIECE, N), F32),
+        out_shape=jax.ShapeDtypeStruct((copies, TILE, N), F32),
         compiler_params=pltpu.CompilerParams(vmem_limit_bytes=32 << 20),
     )(parts)
 
 
-def factor_inverse(gram, scratch):
+def factor_inverse(gram):
     sub = lax.broadcasted_iota(jnp.int32, (TILE, N), 0)
     lane = lax.broadcasted_iota(jnp.int32, (TILE, N), 1)
     work = gram
@@ -184,12 +244,54 @@
     return jnp.concatenate(upper_rows, axis=0), jnp.concatenate(inv_rows, axis=0)
 
 
-def final_kernel(sums_ref, snap_ref, basis_ref, modes_ref, factor_ref, coef_ref, scratch):
-    def pair(i):
-        part = sums_ref[i * TILES : (i + 1) * TILES, :, :]
-        return part[:, :TILE, :].reshape(N, N), part[:, TILE:, :].reshape(N, N)
-
-    basis_gram, cross, snap_gram = pair(0), pair(1), pair(2)
+def three_dot_t(left, right):
+    l1, r1 = left.astype(BF16), right.astype(BF16)
+    l2 = (left - l1.astype(F32)).astype(BF16)
+    r2 = (right - r1.astype(F32)).astype(BF16)
+    return dot_t(jnp.concatenate([l1, l1, l2], 0), jnp.concatenate([r1, r2, r1], 0))
+
+
+def three_dot(left, right):
+    l1, r1 = left.astype(BF16), right.astype(BF16)
+    l2 = (left - l1.astype(F32)).astype(BF16)
+    r2 = (right - r1.astype(F32)).astype(BF16)
+    return dot(jnp.concatenate([l1, l1, l2], 1), jnp.concatenate([r1, r2, r1], 0))
+
+
+NEAR = 2.0**-4
+TURNS = 4
+
+
+def near_factor(off):
+    row, col = grid()
+    weight = jnp.where(row < col, 1.0, jnp.where(row == col, 0.5, 0.0))
+    n = off * weight
+    for _ in range(TURNS):
+        n = (off - three_dot_t(n, n)) * weight
+    eye = jnp.where(row == col, 1.0, 0.0)
+    n2 = three_dot(n, n)
+    n4 = three_dot(n2, n2)
+    inverse = (eye - n) + (n2 - three_dot(n, n2))
+    inverse = inverse + three_dot(inverse, n4)
+    return eye + n, inverse
+
+
+def final_kernel(sums_ref, snap_ref, basis_ref, modes_ref, factor_ref, coef_ref, u_ref, i_ref):
+    row, col = grid()
+    mixed_hi, mixed_lo = unpack(sums_ref[: 2 * TILES])
+    cross = unpack(sums_ref[2 * TILES :])
+    diagonal, mixed_lo = take_diagonal(mixed_lo)
+    turned_hi, turned_lo = mixed_hi.T, mixed_lo.T
+    one = jnp.where(row == col, 1.0, 0.0)
+    one_hi, one_lo = two_sum(one, diagonal)
+    basis_gram = (
+        jnp.where(row == col, one_hi, jnp.where(row < col, mixed_hi, turned_hi)),
+        jnp.where(row == col, one_lo, jnp.where(row < col, mixed_lo, turned_lo)),
+    )
+    snap_gram = (
+        jnp.where(row < col, turned_hi, mixed_hi),
+        jnp.where(row < col, turned_lo, mixed_lo),
+    )
     coef_two = cross[0] - dot(basis_gram[0], cross[0], HIGHEST)
     coef = cross[0] + coef_two
     coef_ref[...] = coef
@@ -202,15 +304,26 @@
     c_h = pair_sum((0.5 * c_h[0], 0.5 * c_h[1]), (0.5 * c_h[0].T, 0.5 * c_h[1].T))
     gram_one = normal(pair_sum(snap_gram, (-c_h[0], -c_h[1])))
 
-    upper_one, inv_one_t = factor_inverse(gram_one[0], scratch)
+    upper_one, inv_one_t = factor_inverse(gram_one[0])
     inv_one = inv_one_t.T
     g_i = exact_dot(slices(*gram_one, 1, 5, 16), slices(inv_one, None, 0, 5, 16))
     g_i = normal(g_i)
     i_g_i = exact_dot(slices(inv_one_t, None, 1, 5, 16), slices(*g_i, 0, 5, 16))
-    gram_two = i_g_i[0] + i_g_i[1]
-    upper_two, inv_two_t = factor_inverse(gram_two, scratch)
-    factor_ref[...] = dot(upper_two, upper_one, HIGHEST)
-    both = dot(inv_one, inv_two_t.T, HIGHEST)
+    off = (i_g_i[0] - one) + i_g_i[1]
+    is_near = jnp.sum(off * off) <= NEAR * NEAR
+
+    @pl.when(is_near)
+    def _():
+        u_ref[...], i_ref[...] = near_factor(off)
+
+    @pl.when(jnp.logical_not(is_near))
+    def _():
+        upper, inv_t = factor_inverse(one + off)
+        u_ref[...] = upper
+        i_ref[...] = inv_t.T
+
+    factor_ref[...] = dot(u_ref[...], upper_one, HIGHEST)
+    both = dot(inv_one, i_ref[...], HIGHEST)
     modes_ref[...] = dot(second, both, HIGHEST)
 
 
@@ -223,14 +336,14 @@
             jax.ShapeDtypeStruct((N, N), F32),
             jax.ShapeDtypeStruct((N, N), F32),
         ),
-        scratch_shapes=[pltpu.VMEM((N, N), F32)],
+        scratch_shapes=[pltpu.VMEM((N, N), F32)] * 2,
         compiler_params=pltpu.CompilerParams(vmem_limit_bytes=48 << 20),
     )(sums, snapshots, basis)
 
 
 def body(snapshots, basis):
     group, many = lax.axis_size("grp"), lax.axis_size("dev")
-    local = local_products(snapshots, basis, many)
+    local = local_products(snapshots, basis, group * many)
     parts = lax.all_to_all(local, "dev", 0, 0)
     mine = sum_and_copy(parts, group)
     parts = lax.all_to_all(mine, "grp", 0, 0)

time: 91.6 us -> 74.9 us (0.82)
  blocking collectives: 70.8 us -> 59.5 us
  Pallas kernels: 18 us -> 12.5 us
    all_to_all x1, blocking collectives: 25 us -> 19.4 us  [body(): sums = lax.all_to_all(mine, 'dev', 0, 0)]
    pallas_call x1, Pallas kernels: 16.9 us -> 11.4 us  [finish(): pl.pallas_call(final_kernel, out_shape=(jax.ShapeDtypeStruct((rows, N), F...]
    all_to_all x1, blocking collectives: 28.7 us -> 23.4 us  [body(): parts = lax.all_to_all(local, 'dev', 0, 0)]
where the time goes in v2:
time: 74.9 us; the launch traced here: 74.6 us
  blocking collectives  59.5 us (79%)
  Pallas kernels  12.5 us (17%)
  local copies, waits for them, and re-layouts  1.91 us (3%)
    all_to_all x1, blocking collectives, body(): parts = lax.all_to_all(local, 'dev', 0, 0)  23.4 us
    all_to_all x1, blocking collectives, body(): sums = lax.all_to_all(mine, 'dev', 0, 0)  19.4 us
    all_to_all x1, blocking collectives, body(): parts = lax.all_to_all(mine, 'grp', 0, 0)  16.7 us
    pallas_call x1, Pallas kernels, finish(): pl.pallas_call(final_kernel, out_shape=(jax.ShapeDtypeStruct((rows, N), F...  11.4 us
    unnamed x8, local copies, waits for them, and re-layouts  1.91 us

profile of v2, /device:TPU:1, one launch (start us, length us, event | category | flops | bytes accessed | tf_op | source)
XLA Modules:
  0.0 74.6 jit_solution(11150856467187497034)
XLA Ops:
  0.6 0.0 copy-start
  0.6 0.9 %copy-done = f32[512,128]{1,0:T(8,128)S(1)} copy-done((f32[512,128]{1,0:T(8,128)S(1)}, f32[512,128]{1,0:T(8,128)}, u32[]{:S(2)}) %copy-start) | copy-done | bytes 262168
  1.6 0.0 copy-start.2
  1.6 0.9 %copy-done.2 = f32[512,128]{1,0:T(8,128)S(1)} copy-done((f32[512,128]{1,0:T(8,128)S(1)}, f32[512,128]{1,0:T(8,128)}, u32[]{:S(2)}) %copy-start.2) | copy-done | bytes 262168
  2.5 1.0 %shard_map.49 = f32[64,8,128]{2,1,0:T(8,128)S(1)} custom-call(f32[512,128]{1,0:T(8,128)S(1)} %copy-done, f32[512,128]{1,0:T(8,128)S(1)} %copy-done.2), custom_call_target="tpu_custom_call" | custom-call | tf_op jit(solution)/shard_map/pallas_call | solution.py:147
  3.6 23.4 %all_to_all.15.in_ref = f32[64,8,128]{2,1,0:T(8,128)S(1)} all-to-all(f32[64,8,128]{2,1,0:T(8,128)S(1)} %shard_map.49), channel_id=1, replica_groups=mesh['grp'=8,'dev'=64] {'dev'}, dimensions={0} | all-to-all | bytes 524288 | tf_op jit(solution)/shard_map/all_to_all | solution.py:347
  27.0 0.1 shard_map.50
  27.1 16.7 %all_to_all.16.in_ref = f32[8,8,128]{2,1,0:T(8,128)S(1)} all-to-all(f32[8,8,128]{2,1,0:T(8,128)S(1)} %shard_map.50), channel_id=1, replica_groups=mesh['grp'=8,'dev'=64] {'grp'}, dimensions={0} | all-to-all | bytes 65536 | tf_op jit(solution)/shard_map/all_to_all | solution.py:349
  43.8 0.0 copy-start.1
  43.8 0.0 copy-start.3
  43.8 19.4 %all_to_all.17.sums_ref = f32[64,8,128]{2,1,0:T(8,128)S(1)} all-to-all(f32[64,8,128]{2,1,0:T(8,128)S(1)} %shard_map.51), channel_id=1, replica_groups=mesh['grp'=8,'dev'=64] {'dev'}, dimensions={0} | all-to-all | bytes 524288 | tf_op jit(solution)/shard_map/all_to_all | solution.py:351
  63.2 0.0 copy-done.1
  63.2 0.0 copy-done.3
  63.2 11.4 %shard_map.52 = (f32[512,128]{1,0:T(8,128)}, f32[128,128]{1,0:T(8,128)}, f32[128,128]{1,0:T(8,128)}) custom-call(f32[64,8,128]{2,1,0:T(8,128)S(1)} %all_to_all.17.sums_ref, f32[512,128]{1,0:T(8,128)S(1)} %copy-done.1, f32[512,128]{1,0:T(8,128)S(1)} %copy-done.3), custom_call_target="tpu_custom_call" | custom-call | tf_op jit(solution)/shard_map/pallas_call | solution.py:332
  (1 shorter events, 0.0 us)
Async XLA Ops:
  0.6 1.0 %copy-start = (f32[512,128]{1,0:T(8,128)S(1)}, f32[512,128]{1,0:T(8,128)}, u32[]{:S(2)}) copy-start(f32[512,128]{1,0:T(8,128)} %snap_ref.1) | copy-start | bytes 786436
  1.6 0.9 %copy-start.2 = (f32[512,128]{1,0:T(8,128)S(1)}, f32[512,128]{1,0:T(8,128)}, u32[]{:S(2)}) copy-start(f32[512,128]{1,0:T(8,128)} %basis_ref.1) | copy-start | bytes 786436
  43.8 19.4 %copy-start.1 = (f32[512,128]{1,0:T(8,128)S(1)}, f32[512,128]{1,0:T(8,128)}, u32[]{:S(2)}) copy-start(f32[512,128]{1,0:T(8,128)} %snap_ref.1) | copy-start | bytes 786436
  43.8 19.4 %copy-start.3 = (f32[512,128]{1,0:T(8,128)S(1)}, f32[512,128]{1,0:T(8,128)}, u32[]{:S(2)}) copy-start(f32[512,128]{1,0:T(8,128)} %basis_ref.1) | copy-start | bytes 786436

commit v3 on v2

--- a/solution.py
+++ b/solution.py
@@ -178,70 +178,54 @@
     )(parts)
 
 
+def spread_row(tile, k):
+    return jnp.broadcast_to(tile[k : k + 1, :], (TILE, N))
+
+
+def spread_lane(tile, j):
+    return jnp.broadcast_to(tile[:, j : j + 1], (TILE, N))
+
+
 def factor_inverse(gram):
     sub = lax.broadcasted_iota(jnp.int32, (TILE, N), 0)
     lane = lax.broadcasted_iota(jnp.int32, (TILE, N), 1)
-    work = gram
-    inv = jnp.where(
-        lax.broadcasted_iota(jnp.int32, (N, N), 0)
-        == lax.broadcasted_iota(jnp.int32, (N, N), 1),
-        1.0,
-        0.0,
-    ).astype(F32)
-    upper_rows, inv_rows = [], []
+    work = [gram[q * TILE : (q + 1) * TILE, :] for q in range(TILES)]
+    upper, inverse = [], []
     for p in range(TILES):
-        at = p * TILE
-        rows = work[:TILE, :]
-        irow = inv[:TILE, :]
+        at, after = p * TILE, range(p + 1, TILES)
         d = {}
         for j in range(TILE):
-            col = jnp.broadcast_to(rows[:, at + j : at + j + 1], (TILE, N))
+            column = spread_lane(work[p], at + j)
             for i in range(j + 1):
-                d[i, j] = jnp.broadcast_to(col[i : i + 1, :], (TILE, N))
-        r = []
+                d[i, j] = spread_row(column, i)
+        below = {(q, j): spread_lane(work[q], at + j) for q in after for j in range(TILE)}
+        right = lane >= at + TILE
+        block = (lane >= at) & (lane < at + TILE)
+        for q in after:
+            work[q] = jnp.where(block, 0.0, work[q])
+        left = jnp.where(lane < at, work[p], jnp.where(lane == at + sub, 1.0, 0.0))
+        rows = [(spread_row(work[p], k), spread_row(left, k)) for k in range(TILE)]
+        new = [jnp.zeros((TILE, N), F32)] * 2
         for k in range(TILE):
-            piv = d[k, k]
-            y = lax.rsqrt(piv)
-            y = y * (1.5 - 0.5 * piv * y * y)
-            r.append(y)
+            scale = lax.rsqrt(d[k, k])
             for j in range(k + 1, TILE):
-                d[k, j] = d[k, j] * y
+                d[k, j] = d[k, j] * scale
             for i in range(k + 1, TILE):
                 for j in range(i, TILE):
                     d[i, j] = d[i, j] - d[k, i] * d[k, j]
-        li = {}
-        for j in range(TILE):
-            li[j, j] = r[j]
-            for i in range(j + 1, TILE):
-                acc = d[j, i] * li[j, j]
-                for k in range(j + 1, i):
-                    acc = acc + d[k, i] * li[k, j]
-                li[i, j] = -(acc * r[i])
-        new_u = jnp.zeros((TILE, N), F32)
-        new_i = jnp.zeros((TILE, N), F32)
-        for k in range(TILE):
-            colk = jnp.zeros((TILE, N), F32)
-            for i in range(k, TILE):
-                colk = jnp.where(sub == i, li[i, k], colk)
-            new_u = new_u + colk * jnp.broadcast_to(rows[k : k + 1, :], (TILE, N))
-            new_i = new_i + colk * jnp.broadcast_to(irow[k : k + 1, :], (TILE, N))
-        new_u = jnp.where(lane >= at + sub, new_u, 0.0)
-        upper_rows.append(new_u)
-        inv_rows.append(new_i)
-        if p + 1 < TILES:
-            both = jnp.concatenate([new_u, new_i], axis=1)
-            b1 = both.astype(BF16)
-            rest = both - b1.astype(F32)
-            b2 = rest.astype(BF16)
-            b3 = (rest - b2.astype(F32)).astype(BF16)
-            f1, f2, f3 = b1.astype(F32), b2.astype(F32), b3.astype(F32)
-            left = jnp.concatenate([f[:, :N] for f in (f1, f1, f2, f1, f2, f3)], axis=0)
-            right = jnp.concatenate([f1, f2, f1, f3, f2, f1], axis=0).astype(BF16)
-            left = left.T.astype(BF16)[at + TILE :, :]
-            upd = dot(left, right)
-            work = work[TILE:, :] - upd[:, :N]
-            inv = inv[TILE:, :] - upd[:, N:]
-    return jnp.concatenate(upper_rows, axis=0), jnp.concatenate(inv_rows, axis=0)
+            row = (rows[k][0] * scale, rows[k][1] * scale)
+            for i in range(k + 1, TILE):
+                rows[i] = tuple(a - d[k, i] * b for a, b in zip(rows[i], row))
+            finished = jnp.where(right, *row)
+            for q in after:
+                m = below[q, k] * scale
+                for j in range(k + 1, TILE):
+                    below[q, j] = below[q, j] - m * d[k, j]
+                work[q] = work[q] - m * finished
+            new = [jnp.where(sub == k, a, b) for a, b in zip(row, new)]
+        upper.append(jnp.where(lane >= at + sub, new[0], 0.0))
+        inverse.append(jnp.where(right, 0.0, new[1]))
+    return jnp.concatenate(upper, axis=0), jnp.concatenate(inverse, axis=0)
 
 
 def three_dot_t(left, right):

time: 74.9 us -> 72.7 us (0.971)
  Pallas kernels: 12.5 us -> 10.3 us
    pallas_call x1, Pallas kernels: 11.4 us -> 9.17 us  [finish(): pl.pallas_call(final_kernel, out_shape=(jax.ShapeDtypeStruct((rows, N), F...]
where the time goes in v3:
time: 72.7 us; the launch traced here: 72.4 us
  blocking collectives  59.5 us (82%)
  Pallas kernels  10.3 us (14%)
  local copies, waits for them, and re-layouts  1.91 us (3%)
    all_to_all x1, blocking collectives, body(): parts = lax.all_to_all(local, 'dev', 0, 0)  23.4 us
    all_to_all x1, blocking collectives, body(): sums = lax.all_to_all(mine, 'dev', 0, 0)  19.4 us
    all_to_all x1, blocking collectives, body(): parts = lax.all_to_all(mine, 'grp', 0, 0)  16.7 us
    pallas_call x1, Pallas kernels, finish(): pl.pallas_call(final_kernel, out_shape=(jax.ShapeDtypeStruct((rows, N), F...  9.17 us
    unnamed x8, local copies, waits for them, and re-layouts  1.91 us

profile of v3, /device:TPU:1, one launch (start us, length us, event | category | flops | bytes accessed | tf_op | source)
XLA Modules:
  0.0 72.4 jit_solution(16423469001247776329)
XLA Ops:
  0.6 0.0 copy-start
  0.6 0.9 %copy-done = f32[512,128]{1,0:T(8,128)S(1)} copy-done((f32[512,128]{1,0:T(8,128)S(1)}, f32[512,128]{1,0:T(8,128)}, u32[]{:S(2)}) %copy-start) | copy-done | bytes 262168
  1.6 0.0 copy-start.2
  1.6 0.9 %copy-done.2 = f32[512,128]{1,0:T(8,128)S(1)} copy-done((f32[512,128]{1,0:T(8,128)S(1)}, f32[512,128]{1,0:T(8,128)}, u32[]{:S(2)}) %copy-start.2) | copy-done | bytes 262168
  2.5 1.0 %shard_map.49 = f32[64,8,128]{2,1,0:T(8,128)S(1)} custom-call(f32[512,128]{1,0:T(8,128)S(1)} %copy-done, f32[512,128]{1,0:T(8,128)S(1)} %copy-done.2), custom_call_target="tpu_custom_call" | custom-call | tf_op jit(solution)/shard_map/pallas_call | solution.py:147
  3.6 23.4 %all_to_all.15.in_ref = f32[64,8,128]{2,1,0:T(8,128)S(1)} all-to-all(f32[64,8,128]{2,1,0:T(8,128)S(1)} %shard_map.49), channel_id=1, replica_groups=mesh['grp'=8,'dev'=64] {'dev'}, dimensions={0} | all-to-all | bytes 524288 | tf_op jit(solution)/shard_map/all_to_all | solution.py:331
  27.0 0.1 shard_map.50
  27.1 16.7 %all_to_all.16.in_ref = f32[8,8,128]{2,1,0:T(8,128)S(1)} all-to-all(f32[8,8,128]{2,1,0:T(8,128)S(1)} %shard_map.50), channel_id=1, replica_groups=mesh['grp'=8,'dev'=64] {'grp'}, dimensions={0} | all-to-all | bytes 65536 | tf_op jit(solution)/shard_map/all_to_all | solution.py:333
  43.8 0.0 copy-start.1
  43.8 0.0 copy-start.3
  43.8 19.4 %all_to_all.17.sums_ref = f32[64,8,128]{2,1,0:T(8,128)S(1)} all-to-all(f32[64,8,128]{2,1,0:T(8,128)S(1)} %shard_map.51), channel_id=1, replica_groups=mesh['grp'=8,'dev'=64] {'dev'}, dimensions={0} | all-to-all | bytes 524288 | tf_op jit(solution)/shard_map/all_to_all | solution.py:335
  63.2 0.0 copy-done.1
  63.2 0.0 copy-done.3
  63.2 9.2 %shard_map.52 = (f32[512,128]{1,0:T(8,128)}, f32[128,128]{1,0:T(8,128)}, f32[128,128]{1,0:T(8,128)}) custom-call(f32[64,8,128]{2,1,0:T(8,128)S(1)} %all_to_all.17.sums_ref, f32[512,128]{1,0:T(8,128)S(1)} %copy-done.1, f32[512,128]{1,0:T(8,128)S(1)} %copy-done.3), custom_call_target="tpu_custom_call" | custom-call | tf_op jit(solution)/shard_map/pallas_call | solution.py:316
  (1 shorter events, 0.0 us)
Async XLA Ops:
  0.6 1.0 %copy-start = (f32[512,128]{1,0:T(8,128)S(1)}, f32[512,128]{1,0:T(8,128)}, u32[]{:S(2)}) copy-start(f32[512,128]{1,0:T(8,128)} %snap_ref.1) | copy-start | bytes 786436
  1.6 0.9 %copy-start.2 = (f32[512,128]{1,0:T(8,128)S(1)}, f32[512,128]{1,0:T(8,128)}, u32[]{:S(2)}) copy-start(f32[512,128]{1,0:T(8,128)} %basis_ref.1) | copy-start | bytes 786436
  43.8 19.4 %copy-start.1 = (f32[512,128]{1,0:T(8,128)S(1)}, f32[512,128]{1,0:T(8,128)}, u32[]{:S(2)}) copy-start(f32[512,128]{1,0:T(8,128)} %snap_ref.1) | copy-start | bytes 786436
  43.8 19.4 %copy-start.3 = (f32[512,128]{1,0:T(8,128)S(1)}, f32[512,128]{1,0:T(8,128)}, u32[]{:S(2)}) copy-start(f32[512,128]{1,0:T(8,128)} %basis_ref.1) | copy-start | bytes 786436

commit v4 on v3

--- a/solution.py
+++ b/solution.py
@@ -5,6 +5,7 @@
 from jax import lax
 from jax.experimental import pallas as pl
 from jax.experimental.pallas import tpu as pltpu
+from jax.sharding import Mesh
 from jax.sharding import PartitionSpec as P
 
 HIGHEST = lax.Precision.HIGHEST
@@ -106,9 +107,7 @@
     return jnp.stack([even, odd], axis=1).reshape(2 * TILES, TILE, N)
 
 
-def unpack(pieces):
-    pieces = pieces.reshape(TILES, 2, TILE, N)
-    even, odd = pieces[:, 0], pieces[:, 1]
+def unpack(even, odd):
     upper = lax.broadcasted_iota(jnp.int32, even.shape, 1) < TILE // 2
     hi = jnp.where(upper, even, pltpu.roll(odd, TILE // 2, 1))
     lo = jnp.where(upper, pltpu.roll(even, TILE // 2, 1), odd)
@@ -246,24 +245,29 @@
 TURNS = 4
 
 
-def near_factor(off):
+def near_factor(off, inv_one):
     row, col = grid()
     weight = jnp.where(row < col, 1.0, jnp.where(row == col, 0.5, 0.0))
     n = off * weight
     for _ in range(TURNS):
         n = (off - three_dot_t(n, n)) * weight
-    eye = jnp.where(row == col, 1.0, 0.0)
+    first = inv_one - dot(inv_one, n, HIGHEST)
     n2 = three_dot(n, n)
-    n4 = three_dot(n2, n2)
-    inverse = (eye - n) + (n2 - three_dot(n, n2))
-    inverse = inverse + three_dot(inverse, n4)
-    return eye + n, inverse
-
-
-def final_kernel(sums_ref, snap_ref, basis_ref, modes_ref, factor_ref, coef_ref, u_ref, i_ref):
+    n2 = n2 + three_dot(n2, n2)
+    return jnp.where(row == col, 1.0, 0.0) + n, first + three_dot(first, n2)
+
+
+PARTS = 4
+
+
+def final_kernel(own_ref, other_ref, snap_ref, basis_ref, modes_hbm, factor_hbm, coef_hbm,
+                 modes_ref, factor_ref, coef_ref, u_ref, t_ref, sem):
     row, col = grid()
-    mixed_hi, mixed_lo = unpack(sums_ref[: 2 * TILES])
-    cross = unpack(sums_ref[2 * TILES :])
+    own, other = own_ref[...], other_ref[...]
+    is_first = lax.axis_index("core") == 0
+    even, odd = jnp.where(is_first, own, other), jnp.where(is_first, other, own)
+    mixed_hi, mixed_lo = unpack(even[:TILES], odd[:TILES])
+    cross = unpack(even[TILES:], odd[TILES:])
     diagonal, mixed_lo = take_diagonal(mixed_lo)
     turned_hi, turned_lo = mixed_hi.T, mixed_lo.T
     one = jnp.where(row == col, 1.0, 0.0)
@@ -279,6 +283,8 @@
     coef_two = cross[0] - dot(basis_gram[0], cross[0], HIGHEST)
     coef = cross[0] + coef_two
     coef_ref[...] = coef
+    coef_copy = pltpu.make_async_copy(coef_ref, coef_hbm, sem.at[0])
+    coef_copy.start()
     second = snap_ref[...] - dot(basis_ref[...], coef, HIGHEST)
 
     g_c = exact_dot(slices(*basis_gram, 1, 5, 16), slices(coef, None, 0, 5, 16))
@@ -296,23 +302,35 @@
     off = (i_g_i[0] - one) + i_g_i[1]
     is_near = jnp.sum(off * off) <= NEAR * NEAR
 
-    @pl.when(is_near)
-    def _():
-        u_ref[...], i_ref[...] = near_factor(off)
+    u_ref[...], t_ref[...] = near_factor(off, inv_one)
 
     @pl.when(jnp.logical_not(is_near))
     def _():
         upper, inv_t = factor_inverse(one + off)
         u_ref[...] = upper
-        i_ref[...] = inv_t.T
-
-    factor_ref[...] = dot(u_ref[...], upper_one, HIGHEST)
-    both = dot(inv_one, i_ref[...], HIGHEST)
-    modes_ref[...] = dot(second, both, HIGHEST)
-
-
-def finish(sums, snapshots, basis):
+        t_ref[...] = dot(inv_one, inv_t.T, HIGHEST)
+
+    both = t_ref[...]
+    copies = [coef_copy]
+    step = modes_ref.shape[0] // PARTS
+    for i in range(PARTS):
+        part = slice(i * step, (i + 1) * step)
+        modes_ref[part, :] = dot(second[part, :], both, HIGHEST)
+        copies.append(
+            pltpu.make_async_copy(modes_ref.at[part, :], modes_hbm.at[part, :], sem.at[2 + i])
+        )
+        copies[-1].start()
+        if i == 0:
+            factor_ref[...] = dot(u_ref[...], upper_one, HIGHEST)
+            copies.append(pltpu.make_async_copy(factor_ref, factor_hbm, sem.at[1]))
+            copies[-1].start()
+    for copy in copies:
+        copy.wait()
+
+
+def finish(own, other, snapshots, basis):
     rows = snapshots.shape[0]
+    square = pltpu.VMEM((N, N), F32)
     return pl.pallas_call(
         final_kernel,
         out_shape=(
@@ -320,27 +338,34 @@
             jax.ShapeDtypeStruct((N, N), F32),
             jax.ShapeDtypeStruct((N, N), F32),
         ),
-        scratch_shapes=[pltpu.VMEM((N, N), F32)] * 2,
+        out_specs=(pl.BlockSpec(memory_space=pltpu.HBM),) * 3,
+        scratch_shapes=[pltpu.VMEM((rows, N), F32)]
+        + [square] * 4
+        + [pltpu.SemaphoreType.DMA((2 + PARTS,))],
         compiler_params=pltpu.CompilerParams(vmem_limit_bytes=48 << 20),
-    )(sums, snapshots, basis)
+    )(own, other, snapshots, basis)
 
 
 def body(snapshots, basis):
-    group, many = lax.axis_size("grp"), lax.axis_size("dev")
-    local = local_products(snapshots, basis, group * many)
-    parts = lax.all_to_all(local, "dev", 0, 0)
+    group, chips, cores = (lax.axis_size(a) for a in ("grp", "chip", "core"))
+    local = local_products(snapshots, basis, group * chips * cores)
+    parts = lax.all_to_all(local, ("chip", "core"), 0, 0)
     mine = sum_and_copy(parts, group)
     parts = lax.all_to_all(mine, "grp", 0, 0)
-    mine = sum_and_copy(parts, many)
-    sums = lax.all_to_all(mine, "dev", 0, 0)
-    return finish(sums, snapshots, basis)
+    mine = sum_and_copy(parts, chips)
+    own = lax.all_to_all(mine, "chip", 0, 0)
+    other = lax.ppermute(own, "core", [(0, 1), (1, 0)])
+    return finish(own, other, snapshots, basis)
 
 
 def solution(mesh):
+    group, many = mesh.devices.shape
+    cores = Mesh(mesh.devices.reshape(group, many // 2, 2), ("grp", "chip", "core"))
+    rows = P(("grp", "chip", "core"), None)
     return jax.shard_map(
         body,
-        mesh=mesh,
-        in_specs=(P(("grp", "dev"), None), P(("grp", "dev"), None)),
-        out_specs=(P(("grp", "dev"), None), P(), P()),
+        mesh=cores,
+        in_specs=(rows, rows),
+        out_specs=(rows, P(), P()),
         check_vma=False,
     )

time: 72.7 us -> 73.6 us (1.012)
  starting transfers between devices: 0 us -> 5.25 us
  blocking collectives: 59.5 us -> 54.4 us
  waiting for transfers between devices: 0 us -> 0.96 us
    all_to_all x2, blocking collectives: 42.8 us -> 37.5 us  [the longest x1 23.4 us: body(): parts = lax.all_to_all(local, ('chip', 'core'), 0, 0)]
    ppermute x0 -> x1, starting transfers between devices: none -> 5.25 us  [body(): other = lax.ppermute(own, 'core', [(0, 1), (1, 0)])]
    ppermute x0 -> x1, waiting for transfers between devices: none -> 0.96 us  [body(): other = lax.ppermute(own, 'core', [(0, 1), (1, 0)])]
  transfers between devices with their start and end apart: 0 -> 1, of which waited for: 0 -> 1; matrix products, arithmetic and copies ran while one was open for 0% -> 0% of each run, Pallas kernels for 0% -> 0%
where the time goes in v4:
time: 73.6 us; the launch traced here: 73.3 us
  blocking collectives  54.4 us (74%)
  Pallas kernels  9.96 us (14%)
  starting transfers between devices  5.25 us (7%)
  local copies, waits for them, and re-layouts  1.9 us (3%)
  waiting for transfers between devices  0.96 us (1%)
  between operations  0.83 us (1%)
    all_to_all x1, blocking collectives, body(): parts = lax.all_to_all(local, ('chip', 'core'), 0, 0)  23.4 us
    all_to_all x1, blocking collectives, body(): parts = lax.all_to_all(mine, 'grp', 0, 0)  16.8 us
    all_to_all x1, blocking collectives, body(): own = lax.all_to_all(mine, 'chip', 0, 0)  14.1 us
    pallas_call x1, Pallas kernels, finish(): pl.pallas_call(final_kernel, out_shape=(jax.ShapeDtypeStruct((rows, N), F...  8.83 us
    ppermute x1, starting transfers between devices, body(): other = lax.ppermute(own, 'core', [(0, 1), (1, 0)])  5.25 us
    unnamed x8, local copies, waits for them, and re-layouts  1.9 us
  transfers between devices with their start and end apart: 1, of which 1 were waited for; matrix products, arithmetic and copies ran while one was open for 0% of the time, Pallas kernels for 0%

profile of v4, /device:TPU:1, one launch (start us, length us, event | category | flops | bytes accessed | tf_op | source)
XLA Modules:
  0.0 73.3 jit_solution(8511389811975460407)
XLA Ops:
  0.6 0.0 copy-start
  0.6 0.9 %copy-done = f32[512,128]{1,0:T(8,128)S(1)} copy-done((f32[512,128]{1,0:T(8,128)S(1)}, f32[512,128]{1,0:T(8,128)}, u32[]{:S(2)}) %copy-start) | copy-done | bytes 262168
  1.6 0.0 copy-start.2
  1.6 0.9 %copy-done.2 = f32[512,128]{1,0:T(8,128)S(1)} copy-done((f32[512,128]{1,0:T(8,128)S(1)}, f32[512,128]{1,0:T(8,128)}, u32[]{:S(2)}) %copy-start.2) | copy-done | bytes 262168
  2.5 1.0 %shard_map.49 = f32[64,8,128]{2,1,0:T(8,128)S(1)} custom-call(f32[512,128]{1,0:T(8,128)S(1)} %copy-done, f32[512,128]{1,0:T(8,128)S(1)} %copy-done.2), custom_call_target="tpu_custom_call" | custom-call | tf_op jit(solution)/shard_map/pallas_call | solution.py:146
  3.6 23.4 %all_to_all.15.in_ref = f32[64,8,128]{2,1,0:T(8,128)S(1)} all-to-all(f32[64,8,128]{2,1,0:T(8,128)S(1)} %shard_map.49), channel_id=1, replica_groups=mesh['grp'=8,'chip'=32,'core'=2] {'chip','core'}, dimensions={0} | all-to-all | bytes 524288 | tf_op jit(solution)/shard_map/all_to_all | solution.py:352
  27.0 0.0 copy-start.3
  27.0 0.1 shard_map.50
  27.1 0.0 copy-start.1
  27.1 16.8 %all_to_all.16.in_ref = f32[8,8,128]{2,1,0:T(8,128)S(1)} all-to-all(f32[8,8,128]{2,1,0:T(8,128)S(1)} %shard_map.50), channel_id=1, replica_groups=mesh['grp'=8,'chip'=32,'core'=2] {'grp'}, dimensions={0} | all-to-all | bytes 65536 | tf_op jit(solution)/shard_map/all_to_all | solution.py:354
  44.0 14.1 %all_to_all.17.own_ref = f32[32,8,128]{2,1,0:T(8,128)S(1)} all-to-all(f32[32,8,128]{2,1,0:T(8,128)S(1)} %shard_map.51), channel_id=1, replica_groups=mesh['grp'=8,'chip'=32,'core'=2] {'chip'}, dimensions={0} | all-to-all | bytes 262144 | tf_op jit(solution)/shard_map/all_to_all | solution.py:356
  58.0 5.3 %collective-permute-start = (f32[32,8,128]{2,1,0:T(8,128)S(1)}, f32[32,8,128]{2,1,0:T(8,128)S(1)}, u32[]{:S(2)}, u32[]{:S(2)}) collective-permute-start(f32[32,8,128]{2,1,0:T(8,128)S(1)} %all_to_all.17.own_ref), channel_id=1, source_target_pairs={{0,1},{1,0},{2,3},{3,2},{4,5},{5,4},{6,7},{7,6},{8,9},{9,8},{10,11... | collective-permute-start | bytes 393224 | tf_op jit(solution)/shard_map/ppermute | solution.py:357
  63.3 1.0 %collective-permute-done.other_ref = f32[32,8,128]{2,1,0:T(8,128)S(1)} collective-permute-done((f32[32,8,128]{2,1,0:T(8,128)S(1)}, f32[32,8,128]{2,1,0:T(8,128)S(1)}, u32[]{:S(2)}, u32[]{:S(2)}) %collective-permute-start) | collective-permute-done | bytes 131104 | tf_op jit(solution)/shard_map/ppermute | solution.py:357
  64.3 0.0 copy-done.3
  64.3 0.0 copy-done.1
  64.3 8.8 %shard_map.52 = (f32[512,128]{1,0:T(8,128)}, f32[128,128]{1,0:T(8,128)}, f32[128,128]{1,0:T(8,128)}) custom-call(f32[32,8,128]{2,1,0:T(8,128)S(1)} %all_to_all.17.own_ref, f32[32,8,128]{2,1,0:T(8,128)S(1)} %collective-permute-done.other_ref, f32[512,128]{1,0:T(8,128)S(1)} %copy-done.1, f32[512,128]{1,0:T(8,128)S(1)} %copy-done.3), custom_call_target="tpu_custom_call" | custom-call | tf_op jit(solution)/shard_map/pallas_call | solution.py:334
  (1 shorter events, 0.0 us)
Async XLA Ops:
  0.6 1.0 %copy-start = (f32[512,128]{1,0:T(8,128)S(1)}, f32[512,128]{1,0:T(8,128)}, u32[]{:S(2)}) copy-start(f32[512,128]{1,0:T(8,128)} %snap_ref.1) | copy-start | bytes 786436
  1.6 0.9 %copy-start.2 = (f32[512,128]{1,0:T(8,128)S(1)}, f32[512,128]{1,0:T(8,128)}, u32[]{:S(2)}) copy-start(f32[512,128]{1,0:T(8,128)} %basis_ref.1) | copy-start | bytes 786436
  27.0 37.3 %copy-start.3 = (f32[512,128]{1,0:T(8,128)S(1)}, f32[512,128]{1,0:T(8,128)}, u32[]{:S(2)}) copy-start(f32[512,128]{1,0:T(8,128)} %basis_ref.1) | copy-start | bytes 786436
  27.1 37.2 %copy-start.1 = (f32[512,128]{1,0:T(8,128)S(1)}, f32[512,128]{1,0:T(8,128)}, u32[]{:S(2)}) copy-start(f32[512,128]{1,0:T(8,128)} %snap_ref.1) | copy-start | bytes 786436
  58.0 6.2 %collective-permute-start = (f32[32,8,128]{2,1,0:T(8,128)S(1)}, f32[32,8,128]{2,1,0:T(8,128)S(1)}, u32[]{:S(2)}, u32[]{:S(2)}) collective-permute-start(f32[32,8,128]{2,1,0:T(8,128)S(1)} %all_to_all.17.own_ref), channel_id=1, source_target_pairs={{0,1},{1,0},{2,3},{3,2},{4,5},{5,4},{6,7},{7,6},{8,9},{9,8},{10,11... | collective-permute-start | bytes 393224 | tf_op jit(solution)/shard_map/ppermute | solution.py:357

commit v5 on v4

--- a/solution.py
+++ b/solution.py
@@ -5,7 +5,6 @@
 from jax import lax
 from jax.experimental import pallas as pl
 from jax.experimental.pallas import tpu as pltpu
-from jax.sharding import Mesh
 from jax.sharding import PartitionSpec as P
 
 HIGHEST = lax.Precision.HIGHEST
@@ -107,22 +106,16 @@
     return jnp.stack([even, odd], axis=1).reshape(2 * TILES, TILE, N)
 
 
-def unpack(even, odd):
+def unpack(pieces):
+    pieces = pieces.reshape(TILES, 2, TILE, N)
+    even, odd = pieces[:, 0], pieces[:, 1]
     upper = lax.broadcasted_iota(jnp.int32, even.shape, 1) < TILE // 2
     hi = jnp.where(upper, even, pltpu.roll(odd, TILE // 2, 1))
     lo = jnp.where(upper, pltpu.roll(even, TILE // 2, 1), odd)
     return hi.reshape(N, N), lo.reshape(N, N)
 
 
-def local_kernel(share, total, snap_hbm, basis_hbm, out_ref, z_ref, sem):
-    copies = [
-        pltpu.make_async_copy(basis_hbm, z_ref.at[:, :N], sem.at[0]),
-        pltpu.make_async_copy(snap_hbm, z_ref.at[:, N:], sem.at[1]),
-    ]
-    for copy in copies:
-        copy.start()
-    for copy in copies:
-        copy.wait()
+def local_kernel(share, total, z_ref, out_ref):
     a, b, c, d = slices(z_ref[...], None, 0, 4, 17)
     main = dot_t(a, a)
     low_1 = dot_t(a, b)
@@ -146,10 +139,8 @@
     return pl.pallas_call(
         functools.partial(local_kernel, 1.0 / devices, total),
         out_shape=jax.ShapeDtypeStruct((4 * TILES, TILE, N), F32),
-        in_specs=[pl.BlockSpec(memory_space=pltpu.HBM)] * 2,
-        scratch_shapes=[pltpu.VMEM((rows, 2 * N), F32), pltpu.SemaphoreType.DMA((2,))],
         compiler_params=pltpu.CompilerParams(vmem_limit_bytes=32 << 20),
-    )(snapshots, basis)
+    )(jnp.concatenate([basis, snapshots], axis=1))
 
 
 def sum_kernel(in_ref, out_ref):
@@ -260,14 +251,11 @@
 PARTS = 4
 
 
-def final_kernel(own_ref, other_ref, snap_ref, basis_ref, modes_hbm, factor_hbm, coef_hbm,
+def final_kernel(sums_ref, snap_ref, basis_ref, modes_hbm, factor_hbm, coef_hbm,
                  modes_ref, factor_ref, coef_ref, u_ref, t_ref, sem):
     row, col = grid()
-    own, other = own_ref[...], other_ref[...]
-    is_first = lax.axis_index("core") == 0
-    even, odd = jnp.where(is_first, own, other), jnp.where(is_first, other, own)
-    mixed_hi, mixed_lo = unpack(even[:TILES], odd[:TILES])
-    cross = unpack(even[TILES:], odd[TILES:])
+    mixed_hi, mixed_lo = unpack(sums_ref[: 2 * TILES])
+    cross = unpack(sums_ref[2 * TILES :])
     diagonal, mixed_lo = take_diagonal(mixed_lo)
     turned_hi, turned_lo = mixed_hi.T, mixed_lo.T
     one = jnp.where(row == col, 1.0, 0.0)
@@ -328,7 +316,7 @@
         copy.wait()
 
 
-def finish(own, other, snapshots, basis):
+def finish(sums, snapshots, basis):
     rows = snapshots.shape[0]
     square = pltpu.VMEM((N, N), F32)
     return pl.pallas_call(
@@ -343,29 +331,25 @@
         + [square] * 4
         + [pltpu.SemaphoreType.DMA((2 + PARTS,))],
         compiler_params=pltpu.CompilerParams(vmem_limit_bytes=48 << 20),
-    )(own, other, snapshots, basis)
+    )(sums, snapshots, basis)
 
 
 def body(snapshots, basis):
-    group, chips, cores = (lax.axis_size(a) for a in ("grp", "chip", "core"))
-    local = local_products(snapshots, basis, group * chips * cores)
-    parts = lax.all_to_all(local, ("chip", "core"), 0, 0)
+    group, many = lax.axis_size("grp"), lax.axis_size("dev")
+    local = local_products(snapshots, basis, group * many)
+    parts = lax.all_to_all(local, "dev", 0, 0)
     mine = sum_and_copy(parts, group)
     parts = lax.all_to_all(mine, "grp", 0, 0)
-    mine = sum_and_copy(parts, chips)
-    own = lax.all_to_all(mine, "chip", 0, 0)
-    other = lax.ppermute(own, "core", [(0, 1), (1, 0)])
-    return finish(own, other, snapshots, basis)
+    mine = sum_and_copy(parts, many)
+    sums = lax.all_to_all(mine, "dev", 0, 0)
+    return finish(sums, snapshots, basis)
 
 
 def solution(mesh):
-    group, many = mesh.devices.shape
-    cores = Mesh(mesh.devices.reshape(group, many // 2, 2), ("grp", "chip", "core"))
-    rows = P(("grp", "chip", "core"), None)
     return jax.shard_map(
         body,
-        mesh=cores,
-        in_specs=(rows, rows),
-        out_specs=(rows, P(), P()),
+        mesh=mesh,
+        in_specs=(P(("grp", "dev"), None), P(("grp", "dev"), None)),
+        out_specs=(P(("grp", "dev"), None), P(), P()),
         check_vma=False,
     )

time: 73.6 us -> 71.6 us (0.973)
  starting transfers between devices: 5.25 us -> 0 us
  blocking collectives: 54.4 us -> 59.5 us
  local copies, waits for them, and re-layouts: 1.9 us -> 0.01 us
  other arithmetic: 0 us -> 1.07 us
  waiting for transfers between devices: 0.96 us -> 0 us
    all_to_all x2, blocking collectives: 37.5 us -> 42.8 us  [the longest x1 23.4 us: body(): parts = lax.all_to_all(local, 'dev', 0, 0)]
    ppermute x1 -> x0, starting transfers between devices: 5.25 us -> none  [body(): other = lax.ppermute(own, 'core', [(0, 1), (1, 0)])]
    unnamed x8 -> x4, local copies, waits for them, and re-layouts: 1.9 us -> 0.01 us
    concatenate x0 -> x1, other arithmetic: none -> 1.07 us  [local_products(): jnp.concatenate([basis, snapshots], axis=1)]
    ppermute x1 -> x0, waiting for transfers between devices: 0.96 us -> none  [body(): other = lax.ppermute(own, 'core', [(0, 1), (1, 0)])]
  transfers between devices with their start and end apart: 1 -> 0, of which waited for: 1 -> 0; matrix products, arithmetic and copies ran while one was open for 0% -> 0% of each run, Pallas kernels for 0% -> 0%
where the time goes in v5:
time: 71.6 us; the launch traced here: 71.3 us
  blocking collectives  59.5 us (83%)
  Pallas kernels  9.92 us (14%)
  other arithmetic  1.07 us (1%)
  between operations  0.82 us (1%)
    all_to_all x1, blocking collectives, body(): parts = lax.all_to_all(local, 'dev', 0, 0)  23.4 us
    all_to_all x1, blocking collectives, body(): sums = lax.all_to_all(mine, 'dev', 0, 0)  19.4 us
    all_to_all x1, blocking collectives, body(): parts = lax.all_to_all(mine, 'grp', 0, 0)  16.7 us
    pallas_call x1, Pallas kernels, finish(): pl.pallas_call(final_kernel, out_shape=(jax.ShapeDtypeStruct((rows, N), F...  8.85 us

profile of v5, /device:TPU:1, one launch (start us, length us, event | category | flops | bytes accessed | tf_op | source)
XLA Modules:
  0.0 71.3 jit_solution(993857794446690822)
XLA Ops:
  0.6 1.1 %pad_maximum_fusion.z_ref = f32[512,256]{1,0:T(8,128)S(1)} fusion(f32[512,128]{1,0:T(8,128)} %snap_ref.1, f32[512,128]{1,0:T(8,128)} %basis_ref.1), kind=kLoop, calls=%fused_computation | loop fusion | flops 131072 | bytes 1048576 | tf_op jit(solution)/shard_map/concatenate | solution.py:143
  1.7 1.0 %shard_map.49 = f32[64,8,128]{2,1,0:T(8,128)S(1)} custom-call(f32[512,256]{1,0:T(8,128)S(1)} %pad_maximum_fusion.z_ref), custom_call_target="tpu_custom_call" | custom-call | tf_op jit(solution)/shard_map/pallas_call | solution.py:139
  2.7 23.4 %all_to_all.15.in_ref = f32[64,8,128]{2,1,0:T(8,128)S(1)} all-to-all(f32[64,8,128]{2,1,0:T(8,128)S(1)} %shard_map.49), channel_id=1, replica_groups=mesh['grp'=8,'dev'=64] {'dev'}, dimensions={0} | all-to-all | bytes 524288 | tf_op jit(solution)/shard_map/all_to_all | solution.py:340
  26.1 0.1 shard_map.50
  26.2 16.7 %all_to_all.16.in_ref = f32[8,8,128]{2,1,0:T(8,128)S(1)} all-to-all(f32[8,8,128]{2,1,0:T(8,128)S(1)} %shard_map.50), channel_id=1, replica_groups=mesh['grp'=8,'dev'=64] {'grp'}, dimensions={0} | all-to-all | bytes 65536 | tf_op jit(solution)/shard_map/all_to_all | solution.py:342
  42.9 0.0 copy-start
  42.9 0.0 copy-start.1
  42.9 19.4 %all_to_all.17.sums_ref = f32[64,8,128]{2,1,0:T(8,128)S(1)} all-to-all(f32[64,8,128]{2,1,0:T(8,128)S(1)} %shard_map.51), channel_id=1, replica_groups=mesh['grp'=8,'dev'=64] {'dev'}, dimensions={0} | all-to-all | bytes 524288 | tf_op jit(solution)/shard_map/all_to_all | solution.py:344
  62.3 0.0 copy-done
  62.3 0.0 copy-done.1
  62.3 8.8 %shard_map.52 = (f32[512,128]{1,0:T(8,128)}, f32[128,128]{1,0:T(8,128)}, f32[128,128]{1,0:T(8,128)}) custom-call(f32[64,8,128]{2,1,0:T(8,128)S(1)} %all_to_all.17.sums_ref, f32[512,128]{1,0:T(8,128)S(1)} %copy-done, f32[512,128]{1,0:T(8,128)S(1)} %copy-done.1), custom_call_target="tpu_custom_call" | custom-call | tf_op jit(solution)/shard_map/pallas_call | solution.py:322
  (1 shorter events, 0.0 us)
Async XLA Ops:
  42.9 19.4 %copy-start = (f32[512,128]{1,0:T(8,128)S(1)}, f32[512,128]{1,0:T(8,128)}, u32[]{:S(2)}) copy-start(f32[512,128]{1,0:T(8,128)} %snap_ref.1) | copy-start | bytes 786436
  42.9 19.4 %copy-start.1 = (f32[512,128]{1,0:T(8,128)S(1)}, f32[512,128]{1,0:T(8,128)}, u32[]{:S(2)}) copy-start(f32[512,128]{1,0:T(8,128)} %basis_ref.1) | copy-start | bytes 786436

commit v6 on v5

--- a/solution.py
+++ b/solution.py
@@ -176,19 +176,27 @@
     return jnp.broadcast_to(tile[:, j : j + 1], (TILE, N))
 
 
-def factor_inverse(gram):
+AHEAD = 1
+
+
+def spread_ref(ref, p, k):
+    return jnp.broadcast_to(ref[p, k : k + 1, :], (TILE, N))
+
+
+def factor_inverse(gram, scr):
     sub = lax.broadcasted_iota(jnp.int32, (TILE, N), 0)
     lane = lax.broadcasted_iota(jnp.int32, (TILE, N), 1)
     work = [gram[q * TILE : (q + 1) * TILE, :] for q in range(TILES)]
     upper, inverse = [], []
     for p in range(TILES):
         at, after = p * TILE, range(p + 1, TILES)
+        near, far = after[:AHEAD], after[AHEAD:]
         d = {}
         for j in range(TILE):
-            column = spread_lane(work[p], at + j)
+            scr[p, TILE * j : TILE * j + TILE, :] = spread_lane(work[p], at + j)
             for i in range(j + 1):
-                d[i, j] = spread_row(column, i)
-        below = {(q, j): spread_lane(work[q], at + j) for q in after for j in range(TILE)}
+                d[i, j] = spread_ref(scr, p, TILE * j + i)
+        below = {(q, j): spread_lane(work[q], at + j) for q in near for j in range(TILE)}
         right = lane >= at + TILE
         block = (lane >= at) & (lane < at + TILE)
         for q in after:
@@ -207,10 +215,13 @@
             for i in range(k + 1, TILE):
                 rows[i] = tuple(a - d[k, i] * b for a, b in zip(rows[i], row))
             finished = jnp.where(right, *row)
-            for q in after:
+            for q in near:
                 m = below[q, k] * scale
                 for j in range(k + 1, TILE):
                     below[q, j] = below[q, j] - m * d[k, j]
+                work[q] = work[q] - m * finished
+            for q in far:
+                m = jnp.take_along_axis(row[0], sub + q * TILE, axis=1)
                 work[q] = work[q] - m * finished
             new = [jnp.where(sub == k, a, b) for a, b in zip(row, new)]
         upper.append(jnp.where(lane >= at + sub, new[0], 0.0))
@@ -218,11 +229,15 @@
     return jnp.concatenate(upper, axis=0), jnp.concatenate(inverse, axis=0)
 
 
-def three_dot_t(left, right):
-    l1, r1 = left.astype(BF16), right.astype(BF16)
-    l2 = (left - l1.astype(F32)).astype(BF16)
-    r2 = (right - r1.astype(F32)).astype(BF16)
-    return dot_t(jnp.concatenate([l1, l1, l2], 0), jnp.concatenate([r1, r2, r1], 0))
+def three_square(a):
+    hi = a.astype(BF16)
+    lo = (a - hi.astype(F32)).astype(BF16)
+    return lax.dot_general(
+        jnp.concatenate([hi, hi, lo], 1),
+        jnp.concatenate([hi, lo, hi], 1),
+        (((1,), (1,)), ((), ())),
+        preferred_element_type=F32,
+    )
 
 
 def three_dot(left, right):
@@ -238,10 +253,11 @@
 
 def near_factor(off, inv_one):
     row, col = grid()
-    weight = jnp.where(row < col, 1.0, jnp.where(row == col, 0.5, 0.0))
-    n = off * weight
+    weight = jnp.where(row > col, 1.0, jnp.where(row == col, 0.5, 0.0))
+    low = off * weight
     for _ in range(TURNS):
-        n = (off - three_dot_t(n, n)) * weight
+        low = (off - three_square(low)) * weight
+    n = low.T
     first = inv_one - dot(inv_one, n, HIGHEST)
     n2 = three_dot(n, n)
     n2 = n2 + three_dot(n2, n2)
@@ -252,7 +268,7 @@
 
 
 def final_kernel(sums_ref, snap_ref, basis_ref, modes_hbm, factor_hbm, coef_hbm,
-                 modes_ref, factor_ref, coef_ref, u_ref, t_ref, sem):
+                 modes_ref, factor_ref, coef_ref, u_ref, t_ref, sem, scr):
     row, col = grid()
     mixed_hi, mixed_lo = unpack(sums_ref[: 2 * TILES])
     cross = unpack(sums_ref[2 * TILES :])
@@ -282,7 +298,7 @@
     c_h = pair_sum((0.5 * c_h[0], 0.5 * c_h[1]), (0.5 * c_h[0].T, 0.5 * c_h[1].T))
     gram_one = normal(pair_sum(snap_gram, (-c_h[0], -c_h[1])))
 
-    upper_one, inv_one_t = factor_inverse(gram_one[0])
+    upper_one, inv_one_t = factor_inverse(gram_one[0], scr)
     inv_one = inv_one_t.T
     g_i = exact_dot(slices(*gram_one, 1, 5, 16), slices(inv_one, None, 0, 5, 16))
     g_i = normal(g_i)
@@ -294,7 +310,7 @@
 
     @pl.when(jnp.logical_not(is_near))
     def _():
-        upper, inv_t = factor_inverse(one + off)
+        upper, inv_t = factor_inverse(one + off, scr)
         u_ref[...] = upper
         t_ref[...] = dot(inv_one, inv_t.T, HIGHEST)
 
@@ -329,7 +345,7 @@
         out_specs=(pl.BlockSpec(memory_space=pltpu.HBM),) * 3,
         scratch_shapes=[pltpu.VMEM((rows, N), F32)]
         + [square] * 4
-        + [pltpu.SemaphoreType.DMA((2 + PARTS,))],
+        + [pltpu.SemaphoreType.DMA((2 + PARTS,)), pltpu.VMEM((TILES, TILE * TILE, N), F32)],
         compiler_params=pltpu.CompilerParams(vmem_limit_bytes=48 << 20),
     )(sums, snapshots, basis)
 

time: 71.6 us -> 69.7 us (0.973)
  Pallas kernels: 9.92 us -> 8.23 us
    pallas_call x1, Pallas kernels: 8.85 us -> 7.16 us  [finish(): pl.pallas_call(final_kernel, out_shape=(jax.ShapeDtypeStruct((rows, N), F...]
where the time goes in v6:
time: 69.7 us; the launch traced here: 69.5 us
  blocking collectives  59.5 us (85%)
  Pallas kernels  8.23 us (12%)
  other arithmetic  1.07 us (2%)
    all_to_all x1, blocking collectives, body(): parts = lax.all_to_all(local, 'dev', 0, 0)  23.4 us
    all_to_all x1, blocking collectives, body(): sums = lax.all_to_all(mine, 'dev', 0, 0)  19.4 us
    all_to_all x1, blocking collectives, body(): parts = lax.all_to_all(mine, 'grp', 0, 0)  16.7 us
    pallas_call x1, Pallas kernels, finish(): pl.pallas_call(final_kernel, out_shape=(jax.ShapeDtypeStruct((rows, N), F...  7.16 us

profile of v6, /device:TPU:1, one launch (start us, length us, event | category | flops | bytes accessed | tf_op | source)
XLA Modules:
  0.0 69.5 jit_solution(7944266084284295138)
XLA Ops:
  0.6 1.1 %pad_maximum_fusion.z_ref = f32[512,256]{1,0:T(8,128)S(1)} fusion(f32[512,128]{1,0:T(8,128)} %snap_ref.1, f32[512,128]{1,0:T(8,128)} %basis_ref.1), kind=kLoop, calls=%fused_computation | loop fusion | flops 131072 | bytes 1048576 | tf_op jit(solution)/shard_map/concatenate | solution.py:143
  1.7 1.0 %shard_map.49 = f32[64,8,128]{2,1,0:T(8,128)S(1)} custom-call(f32[512,256]{1,0:T(8,128)S(1)} %pad_maximum_fusion.z_ref), custom_call_target="tpu_custom_call" | custom-call | tf_op jit(solution)/shard_map/pallas_call | solution.py:139
  2.7 23.4 %all_to_all.15.in_ref = f32[64,8,128]{2,1,0:T(8,128)S(1)} all-to-all(f32[64,8,128]{2,1,0:T(8,128)S(1)} %shard_map.49), channel_id=1, replica_groups=mesh['grp'=8,'dev'=64] {'dev'}, dimensions={0} | all-to-all | bytes 524288 | tf_op jit(solution)/shard_map/all_to_all | solution.py:356
  26.1 0.1 shard_map.50
  26.2 16.7 %all_to_all.16.in_ref = f32[8,8,128]{2,1,0:T(8,128)S(1)} all-to-all(f32[8,8,128]{2,1,0:T(8,128)S(1)} %shard_map.50), channel_id=1, replica_groups=mesh['grp'=8,'dev'=64] {'grp'}, dimensions={0} | all-to-all | bytes 65536 | tf_op jit(solution)/shard_map/all_to_all | solution.py:358
  42.9 0.0 copy-start
  42.9 0.0 copy-start.1
  42.9 19.4 %all_to_all.17.sums_ref = f32[64,8,128]{2,1,0:T(8,128)S(1)} all-to-all(f32[64,8,128]{2,1,0:T(8,128)S(1)} %shard_map.51), channel_id=1, replica_groups=mesh['grp'=8,'dev'=64] {'dev'}, dimensions={0} | all-to-all | bytes 524288 | tf_op jit(solution)/shard_map/all_to_all | solution.py:360
  62.3 0.0 copy-done
  62.3 0.0 copy-done.1
  62.3 7.2 %shard_map.52 = (f32[512,128]{1,0:T(8,128)}, f32[128,128]{1,0:T(8,128)}, f32[128,128]{1,0:T(8,128)}) custom-call(f32[64,8,128]{2,1,0:T(8,128)S(1)} %all_to_all.17.sums_ref, f32[512,128]{1,0:T(8,128)S(1)} %copy-done, f32[512,128]{1,0:T(8,128)S(1)} %copy-done.1), custom_call_target="tpu_custom_call" | custom-call | tf_op jit(solution)/shard_map/pallas_call | solution.py:338
  (1 shorter events, 0.0 us)
Async XLA Ops:
  42.9 19.4 %copy-start = (f32[512,128]{1,0:T(8,128)S(1)}, f32[512,128]{1,0:T(8,128)}, u32[]{:S(2)}) copy-start(f32[512,128]{1,0:T(8,128)} %snap_ref.1) | copy-start | bytes 786436
  42.9 19.4 %copy-start.1 = (f32[512,128]{1,0:T(8,128)S(1)}, f32[512,128]{1,0:T(8,128)}, u32[]{:S(2)}) copy-start(f32[512,128]{1,0:T(8,128)} %basis_ref.1) | copy-start | bytes 786436

commit v7 on v6

--- a/solution.py
+++ b/solution.py
@@ -229,6 +229,17 @@
     return jnp.concatenate(upper, axis=0), jnp.concatenate(inverse, axis=0)
 
 
+def power_near(value):
+    p, q = jnp.ones_like(value), jnp.ones_like(value)
+    for k in (4, 2, 1):
+        large = (value * p) * p > 2.0 ** (2 * k - 1)
+        p, q = jnp.where(large, p * 2.0**-k, p), jnp.where(large, q * 2.0**k, q)
+    for k in (32, 16, 8, 4, 2, 1):
+        small = (value * p) * p < 2.0 ** (1 - 2 * k)
+        p, q = jnp.where(small, p * 2.0**k, p), jnp.where(small, q * 2.0**-k, q)
+    return p, q
+
+
 def three_square(a):
     hi = a.astype(BF16)
     lo = (a - hi.astype(F32)).astype(BF16)
@@ -300,9 +311,13 @@
 
     upper_one, inv_one_t = factor_inverse(gram_one[0], scr)
     inv_one = inv_one_t.T
-    g_i = exact_dot(slices(*gram_one, 1, 5, 16), slices(inv_one, None, 0, 5, 16))
+    diagonal = jnp.where(row == col, gram_one[0], 0.0)
+    across, back_across = power_near(jnp.sum(diagonal, axis=0, keepdims=True))
+    down, back_down = power_near(jnp.sum(diagonal, axis=1, keepdims=True))
+    scaled = tuple((part * across) * down for part in gram_one)
+    g_i = exact_dot(slices(*scaled, 1, 5, 16), slices(inv_one * back_down, None, 0, 5, 16))
     g_i = normal(g_i)
-    i_g_i = exact_dot(slices(inv_one_t, None, 1, 5, 16), slices(*g_i, 0, 5, 16))
+    i_g_i = exact_dot(slices(inv_one_t * back_across, None, 1, 5, 16), slices(*g_i, 0, 5, 16))
     off = (i_g_i[0] - one) + i_g_i[1]
     is_near = jnp.sum(off * off) <= NEAR * NEAR
 

time: 69.7 us -> 69.8 us (level)
  no operation moved by 1% of the time
where the time goes in v7:
time: 69.8 us; the launch traced here: 69.6 us
  blocking collectives  59.5 us (85%)
  Pallas kernels  8.31 us (12%)
  other arithmetic  1.07 us (2%)
    all_to_all x1, blocking collectives, body(): parts = lax.all_to_all(local, 'dev', 0, 0)  23.4 us
    all_to_all x1, blocking collectives, body(): sums = lax.all_to_all(mine, 'dev', 0, 0)  19.4 us
    all_to_all x1, blocking collectives, body(): parts = lax.all_to_all(mine, 'grp', 0, 0)  16.7 us
    pallas_call x1, Pallas kernels, finish(): pl.pallas_call(final_kernel, out_shape=(jax.ShapeDtypeStruct((rows, N), F...  7.24 us

profile of v7, /device:TPU:1, one launch (start us, length us, event | category | flops | bytes accessed | tf_op | source)
XLA Modules:
  0.0 69.6 jit_solution(7824415335790007768)
XLA Ops:
  0.6 1.1 %pad_maximum_fusion.z_ref = f32[512,256]{1,0:T(8,128)S(1)} fusion(f32[512,128]{1,0:T(8,128)} %snap_ref.1, f32[512,128]{1,0:T(8,128)} %basis_ref.1), kind=kLoop, calls=%fused_computation | loop fusion | flops 131072 | bytes 1048576 | tf_op jit(solution)/shard_map/concatenate | solution.py:143
  1.7 1.0 %shard_map.49 = f32[64,8,128]{2,1,0:T(8,128)S(1)} custom-call(f32[512,256]{1,0:T(8,128)S(1)} %pad_maximum_fusion.z_ref), custom_call_target="tpu_custom_call" | custom-call | tf_op jit(solution)/shard_map/pallas_call | solution.py:139
  2.7 23.4 %all_to_all.15.in_ref = f32[64,8,128]{2,1,0:T(8,128)S(1)} all-to-all(f32[64,8,128]{2,1,0:T(8,128)S(1)} %shard_map.49), channel_id=1, replica_groups=mesh['grp'=8,'dev'=64] {'dev'}, dimensions={0} | all-to-all | bytes 524288 | tf_op jit(solution)/shard_map/all_to_all | solution.py:371
  26.1 0.1 shard_map.50
  26.2 16.7 %all_to_all.16.in_ref = f32[8,8,128]{2,1,0:T(8,128)S(1)} all-to-all(f32[8,8,128]{2,1,0:T(8,128)S(1)} %shard_map.50), channel_id=1, replica_groups=mesh['grp'=8,'dev'=64] {'grp'}, dimensions={0} | all-to-all | bytes 65536 | tf_op jit(solution)/shard_map/all_to_all | solution.py:373
  42.9 0.0 copy-start
  42.9 0.0 copy-start.1
  42.9 19.4 %all_to_all.17.sums_ref = f32[64,8,128]{2,1,0:T(8,128)S(1)} all-to-all(f32[64,8,128]{2,1,0:T(8,128)S(1)} %shard_map.51), channel_id=1, replica_groups=mesh['grp'=8,'dev'=64] {'dev'}, dimensions={0} | all-to-all | bytes 524288 | tf_op jit(solution)/shard_map/all_to_all | solution.py:375
  62.3 0.0 copy-done
  62.3 0.0 copy-done.1
  62.3 7.2 %shard_map.52 = (f32[512,128]{1,0:T(8,128)}, f32[128,128]{1,0:T(8,128)}, f32[128,128]{1,0:T(8,128)}) custom-call(f32[64,8,128]{2,1,0:T(8,128)S(1)} %all_to_all.17.sums_ref, f32[512,128]{1,0:T(8,128)S(1)} %copy-done, f32[512,128]{1,0:T(8,128)S(1)} %copy-done.1), custom_call_target="tpu_custom_call" | custom-call | tf_op jit(solution)/shard_map/pallas_call | solution.py:353
  (1 shorter events, 0.0 us)
Async XLA Ops:
  42.9 19.4 %copy-start = (f32[512,128]{1,0:T(8,128)S(1)}, f32[512,128]{1,0:T(8,128)}, u32[]{:S(2)}) copy-start(f32[512,128]{1,0:T(8,128)} %snap_ref.1) | copy-start | bytes 786436
  42.9 19.4 %copy-start.1 = (f32[512,128]{1,0:T(8,128)S(1)}, f32[512,128]{1,0:T(8,128)}, u32[]{:S(2)}) copy-start(f32[512,128]{1,0:T(8,128)} %basis_ref.1) | copy-start | bytes 786436

commit v8 on v7

--- a/solution.py
+++ b/solution.py
@@ -202,7 +202,12 @@
         for q in after:
             work[q] = jnp.where(block, 0.0, work[q])
         left = jnp.where(lane < at, work[p], jnp.where(lane == at + sub, 1.0, 0.0))
-        rows = [(spread_row(work[p], k), spread_row(left, k)) for k in range(TILE)]
+        scr[p, TILE * TILE : TILE * TILE + TILE, :] = work[p]
+        scr[p, TILE * TILE + TILE :, :] = left
+        rows = [
+            (spread_ref(scr, p, TILE * TILE + k), spread_ref(scr, p, TILE * TILE + TILE + k))
+            for k in range(TILE)
+        ]
         new = [jnp.zeros((TILE, N), F32)] * 2
         for k in range(TILE):
             scale = lax.rsqrt(d[k, k])
@@ -360,7 +365,7 @@
         out_specs=(pl.BlockSpec(memory_space=pltpu.HBM),) * 3,
         scratch_shapes=[pltpu.VMEM((rows, N), F32)]
         + [square] * 4
-        + [pltpu.SemaphoreType.DMA((2 + PARTS,)), pltpu.VMEM((TILES, TILE * TILE, N), F32)],
+        + [pltpu.SemaphoreType.DMA((2 + PARTS,)), pltpu.VMEM((TILES, TILE * (TILE + 2), N), F32)],
         compiler_params=pltpu.CompilerParams(vmem_limit_bytes=48 << 20),
     )(sums, snapshots, basis)
 

time: 69.8 us -> 69.8 us (level)
  no operation moved by 1% of the time
where the time goes in v8:
time: 69.8 us; the launch traced here: 69.6 us
  blocking collectives  59.5 us (85%)
  Pallas kernels  8.31 us (12%)
  other arithmetic  1.07 us (2%)
    all_to_all x1, blocking collectives, body(): parts = lax.all_to_all(local, 'dev', 0, 0)  23.4 us
    all_to_all x1, blocking collectives, body(): sums = lax.all_to_all(mine, 'dev', 0, 0)  19.4 us
    all_to_all x1, blocking collectives, body(): parts = lax.all_to_all(mine, 'grp', 0, 0)  16.7 us
    pallas_call x1, Pallas kernels, finish(): pl.pallas_call(final_kernel, out_shape=(jax.ShapeDtypeStruct((rows, N), F...  7.24 us

profile of v8, /device:TPU:1, one launch (start us, length us, event | category | flops | bytes accessed | tf_op | source)
XLA Modules:
  0.0 69.6 jit_solution(17945433806689627844)
XLA Ops:
  0.6 1.1 %pad_maximum_fusion.z_ref = f32[512,256]{1,0:T(8,128)S(1)} fusion(f32[512,128]{1,0:T(8,128)} %snap_ref.1, f32[512,128]{1,0:T(8,128)} %basis_ref.1), kind=kLoop, calls=%fused_computation | loop fusion | flops 131072 | bytes 1048576 | tf_op jit(solution)/shard_map/concatenate | solution.py:143
  1.7 1.0 %shard_map.49 = f32[64,8,128]{2,1,0:T(8,128)S(1)} custom-call(f32[512,256]{1,0:T(8,128)S(1)} %pad_maximum_fusion.z_ref), custom_call_target="tpu_custom_call" | custom-call | tf_op jit(solution)/shard_map/pallas_call | solution.py:139
  2.7 23.4 %all_to_all.15.in_ref = f32[64,8,128]{2,1,0:T(8,128)S(1)} all-to-all(f32[64,8,128]{2,1,0:T(8,128)S(1)} %shard_map.49), channel_id=1, replica_groups=mesh['grp'=8,'dev'=64] {'dev'}, dimensions={0} | all-to-all | bytes 524288 | tf_op jit(solution)/shard_map/all_to_all | solution.py:376
  26.1 0.1 shard_map.50
  26.2 16.7 %all_to_all.16.in_ref = f32[8,8,128]{2,1,0:T(8,128)S(1)} all-to-all(f32[8,8,128]{2,1,0:T(8,128)S(1)} %shard_map.50), channel_id=1, replica_groups=mesh['grp'=8,'dev'=64] {'grp'}, dimensions={0} | all-to-all | bytes 65536 | tf_op jit(solution)/shard_map/all_to_all | solution.py:378
  42.9 0.0 copy-start
  42.9 0.0 copy-start.1
  42.9 19.4 %all_to_all.17.sums_ref = f32[64,8,128]{2,1,0:T(8,128)S(1)} all-to-all(f32[64,8,128]{2,1,0:T(8,128)S(1)} %shard_map.51), channel_id=1, replica_groups=mesh['grp'=8,'dev'=64] {'dev'}, dimensions={0} | all-to-all | bytes 524288 | tf_op jit(solution)/shard_map/all_to_all | solution.py:380
  62.3 0.0 copy-done
  62.3 0.0 copy-done.1
  62.3 7.2 %shard_map.52 = (f32[512,128]{1,0:T(8,128)}, f32[128,128]{1,0:T(8,128)}, f32[128,128]{1,0:T(8,128)}) custom-call(f32[64,8,128]{2,1,0:T(8,128)S(1)} %all_to_all.17.sums_ref, f32[512,128]{1,0:T(8,128)S(1)} %copy-done, f32[512,128]{1,0:T(8,128)S(1)} %copy-done.1), custom_call_target="tpu_custom_call" | custom-call | tf_op jit(solution)/shard_map/pallas_call | solution.py:358
  (1 shorter events, 0.0 us)
Async XLA Ops:
  42.9 19.4 %copy-start = (f32[512,128]{1,0:T(8,128)S(1)}, f32[512,128]{1,0:T(8,128)}, u32[]{:S(2)}) copy-start(f32[512,128]{1,0:T(8,128)} %snap_ref.1) | copy-start | bytes 786436
  42.9 19.4 %copy-start.1 = (f32[512,128]{1,0:T(8,128)S(1)}, f32[512,128]{1,0:T(8,128)}, u32[]{:S(2)}) copy-start(f32[512,128]{1,0:T(8,128)} %basis_ref.1) | copy-start | bytes 786436
